TPU v7x, 128 devices: a whole 4x4x4 slice. The times are simulated.
128 devices in a mesh: ctx: 32 (over x, y, z_hi), fsdp: 4 (over z_lo, core).
Axes of the slice: x: 4, y: 4, z: 4 (z_hi: 2, z_lo: 2; z = z_hi * 2 + z_lo), core: 2. Of those that a mesh axis runs over, the one named last changes fastest.
Arguments:
- hidden_in: bfloat16 [4, 4096, 1024], P('fsdp', 'ctx'), may hold values from -6 to 6
- cotangent: bfloat16 [4, 4096, 1024], P('fsdp', 'ctx'), may hold values from -6 to 6
- pair_table: int32 [32], replicated, may hold values from 0 to 31, each once
- norm_gain: bfloat16 [2, 2, 1024], P(None, None, 'fsdp'), may hold values from 0.5 to 1.5
- norm_bias: bfloat16 [2, 2, 1024], P(None, None, 'fsdp'), may hold values from -1.75 to 1.75
- qkv_weight: bfloat16 [2, 1024, 3072], P(None, 'fsdp'), may hold values from -0.1875 to 0.1875
- qkv_bias: bfloat16 [2, 3072], P(None, 'fsdp'), may hold values from -3 to 3
- out_weight: bfloat16 [2, 1024, 1024], P(None, 'fsdp'), may hold values from -4 to 4
- out_bias: bfloat16 [2, 1024], P(None, 'fsdp'), may hold values from -3 to 3
- up_weight: bfloat16 [2, 1024, 4096], P(None, 'fsdp'), may hold values from -0.1875 to 0.1875
- up_bias: bfloat16 [2, 4096], P(None, 'fsdp'), may hold values from -3 to 3
- down_weight: bfloat16 [2, 4096, 1024], P(None, 'fsdp'), may hold values from -0.09375 to 0.09375
- down_bias: bfloat16 [2, 1024], P(None, 'fsdp'), may hold values from -3 to 3
Outputs:
- hidden_out: bfloat16 [4, 4096, 1024], P('fsdp', 'ctx')
- input_grad: float32 [4, 4096, 1024], P('fsdp', 'ctx')
- norm_gain_grad: float32 [2, 2, 1024], P(None, None, 'fsdp')
- norm_bias_grad: float32 [2, 2, 1024], P(None, None, 'fsdp')
- qkv_weight_grad: float32 [2, 1024, 3072], P(None, 'fsdp')
- qkv_bias_grad: float32 [2, 3072], P(None, 'fsdp')
- out_weight_grad: float32 [2, 1024, 1024], P(None, 'fsdp')
- out_bias_grad: float32 [2, 1024], P(None, 'fsdp')
- up_weight_grad: float32 [2, 1024, 4096], P(None, 'fsdp')
- up_bias_grad: float32 [2, 4096], P(None, 'fsdp')
- down_weight_grad: float32 [2, 4096, 1024], P(None, 'fsdp')
- down_bias_grad: float32 [2, 1024], P(None, 'fsdp')
Inputs may be any that keep to these rules, and one draw needn't show every extreme that they name: pair_table is a permutation of the 32 block pairs; slot c holds pair pair_table[c].
All inputs are finite; a program needn't handle non-finite values.
Results may differ from a plain program's by a relative error of at most 0.025.
Values may be sent and summed in bfloat16 or wider, within the bound.
A program may use at most 384 MiB of HBM per device.

v0:
```python
import jax
import jax.numpy as jnp
from jax import lax
from jax.sharding import PartitionSpec as P

HEADS = 16


EPS = 1e-05
NEGATIVE = -1e30


def pair_positions(pair_table, block_len):
    slots = pair_table.shape[0]
    blocks = jnp.stack([pair_table, 2 * slots - 1 - pair_table], 1)
    within = jnp.arange(block_len, dtype=jnp.int32)
    return (blocks[:, :, None] * block_len + within[None, None, :]).reshape(-1)


def rotation(positions, rot_dims):
    freqs = 10000.0 ** (-jnp.arange(0, rot_dims, 2, dtype=jnp.float32) / rot_dims)
    angles = positions.astype(jnp.float32)[:, None] * freqs[None, :]
    return (jnp.concatenate([jnp.cos(angles)] * 2, -1), jnp.concatenate([jnp.sin(angles)] * 2, -1))


def rope(inputs, cosines, sines):
    rot_dims = cosines.shape[-1]
    half_dims = rot_dims // 2
    turning = inputs[..., :rot_dims]
    turned = jnp.concatenate([-turning[..., half_dims:], turning[..., :half_dims]], -1)
    rotated = turning * cosines[:, None, :] + turned * sines[:, None, :]
    return jnp.concatenate([rotated, inputs[..., rot_dims:]], -1)


def standardize(stream):
    row_mean = jnp.mean(stream, -1, keepdims=True)
    centered = stream - row_mean
    spread = jnp.mean(centered * centered, -1, keepdims=True)
    inverse = lax.rsqrt(spread + EPS)
    return (centered * inverse, inverse)


def outer_sum(inputs, output_grad):
    return lax.dot_general(
        inputs, output_grad, (((0,), (0,)), ((), ())), preferred_element_type=jnp.float32
    )


def against(output_grad, matrix):
    return lax.dot_general(
        output_grad, matrix, (((1,), (1,)), ((), ())), preferred_element_type=jnp.float32
    )


def gelu_exact(inputs):
    return jax.nn.gelu(inputs, approximate=False)


def key_blocks(keys_all, values_all, key_pos, block_rows, head_count):
    key_total, model_width = keys_all.shape
    block_count = key_total // block_rows
    block_shape = (block_count, block_rows, head_count, model_width // head_count)
    return (
        keys_all.reshape(block_shape),
        values_all.reshape(block_shape),
        key_pos.reshape(block_count, block_rows),
    )


def attend(queries, keys_all, values_all, query_pos, key_pos, block_rows):
    row_count, head_count, head_size = queries.shape
    score_scale = head_size ** (-0.5)
    blocks = key_blocks(keys_all, values_all, key_pos, block_rows, head_count)

    def step(carry, key_block):
        row_max, row_sum, weighted = carry
        keys_part, values_part, pos_part = key_block
        scores = (
            jnp.einsum("qhe,khe->hqk", queries, keys_part, preferred_element_type=jnp.float32)
            * score_scale
        )
        allowed = pos_part[None, None, :] <= query_pos[None, :, None]
        scores = jnp.where(allowed, scores, NEGATIVE)
        new_max = jnp.maximum(row_max, jnp.max(scores, -1, keepdims=True))
        weights = jnp.where(allowed, jnp.exp(scores - new_max), 0.0)
        rescale = jnp.exp(row_max - new_max)
        row_sum = row_sum * rescale + jnp.sum(weights, -1, keepdims=True)
        weighted = weighted * rescale + jnp.einsum(
            "hqk,khe->hqe",
            weights.astype(jnp.bfloat16),
            values_part,
            preferred_element_type=jnp.float32,
        )
        return ((new_max, row_sum, weighted), None)

    initial = (
        jnp.full((head_count, row_count, 1), NEGATIVE, jnp.float32),
        jnp.zeros((head_count, row_count, 1), jnp.float32),
        jnp.zeros((head_count, row_count, head_size), jnp.float32),
    )
    (row_max, row_sum, weighted), unused = lax.scan(step, initial, blocks)
    context = jnp.transpose(weighted / row_sum, (1, 0, 2))
    return (context, row_max + jnp.log(row_sum))


def attend_back(
    queries, keys_all, values_all, query_pos, key_pos, block_rows, log_total, offsets, context_grad
):
    row_count, head_count, head_size = queries.shape
    score_scale = head_size ** (-0.5)
    blocks = key_blocks(keys_all, values_all, key_pos, block_rows, head_count)

    def step(query_grad, key_block):
        keys_part, values_part, pos_part = key_block
        scores = (
            jnp.einsum("qhe,khe->hqk", queries, keys_part, preferred_element_type=jnp.float32)
            * score_scale
        )
        allowed = pos_part[None, None, :] <= query_pos[None, :, None]
        scores = jnp.where(allowed, scores, NEGATIVE)
        probs = jnp.exp(scores - log_total)
        prob_grad = jnp.einsum(
            "qhe,khe->hqk", context_grad, values_part, preferred_element_type=jnp.float32
        )
        score_grad = (probs * (prob_grad - offsets)).astype(jnp.bfloat16)
        query_grad = query_grad + jnp.einsum(
            "hqk,khe->qhe", score_grad, keys_part, preferred_element_type=jnp.float32
        )
        key_grad = (
            jnp.einsum("hqk,qhe->khe", score_grad, queries, preferred_element_type=jnp.float32)
            * score_scale
        )
        value_grad = jnp.einsum(
            "hqk,qhe->khe",
            probs.astype(jnp.bfloat16),
            context_grad,
            preferred_element_type=jnp.float32,
        )
        return (query_grad, (key_grad, value_grad))

    query_grad, key_parts = lax.scan(
        step, jnp.zeros((row_count, head_count, head_size), jnp.float32), blocks
    )
    key_total = keys_all.shape[0]
    return (
        query_grad * score_scale,
        key_parts[0].reshape(key_total, -1),
        key_parts[1].reshape(key_total, -1),
    )


def layer_forward(stream, weights, cosines, sines, query_pos, key_pos, block_rows, head_count):
    gain, shift, w_qkv, b_qkv, w_out, b_out, w_up, b_up, w_down, b_down = weights
    row_count, model_width = stream.shape
    head_size = model_width // head_count
    normed, inverse = standardize(stream)
    gain_full = gain.astype(jnp.float32)
    shift_full = shift.astype(jnp.float32)
    first = (normed * gain_full[0] + shift_full[0]).astype(jnp.bfloat16)
    second = (normed * gain_full[1] + shift_full[1]).astype(jnp.bfloat16)
    mixed = jnp.dot(first, w_qkv, preferred_element_type=jnp.float32) + b_qkv.astype(jnp.float32)
    queries = rope(
        mixed[:, :model_width].reshape(row_count, head_count, head_size), cosines, sines
    ).astype(jnp.bfloat16)
    keys_own = (
        rope(
            mixed[:, model_width : 2 * model_width].reshape(row_count, head_count, head_size),
            cosines,
            sines,
        )
        .astype(jnp.bfloat16)
        .reshape(row_count, model_width)
    )
    values_own = mixed[:, 2 * model_width :].astype(jnp.bfloat16)
    keys_all, values_all = (
        lax.all_gather(keys_own, "ctx", axis=0, tiled=True),
        lax.all_gather(values_own, "ctx", axis=0, tiled=True),
    )
    context, log_total = attend(queries, keys_all, values_all, query_pos, key_pos, block_rows)
    context_low = context.reshape(row_count, model_width).astype(jnp.bfloat16)
    attn_out = jnp.dot(context_low, w_out, preferred_element_type=jnp.float32) + b_out.astype(
        jnp.float32
    )
    hidden = jnp.dot(second, w_up, preferred_element_type=jnp.float32) + b_up.astype(jnp.float32)
    active = gelu_exact(hidden).astype(jnp.bfloat16)
    mlp_out = jnp.dot(active, w_down, preferred_element_type=jnp.float32) + b_down.astype(
        jnp.float32
    )
    saved = (
        normed,
        inverse,
        first,
        second,
        queries,
        keys_own,
        values_own,
        keys_all,
        values_all,
        context,
        log_total,
        context_low,
        hidden,
        active,
    )
    return (stream + attn_out + mlp_out, saved)


def layer_backward(
    stream_grad,
    weights,
    saved,
    keys_all,
    values_all,
    cosines,
    sines,
    query_pos,
    key_pos,
    block_rows,
    head_count,
):
    gain, shift, w_qkv, b_qkv, w_out, b_out, w_up, b_up, w_down, b_down = weights
    normed, inverse, first, second, queries = (saved[0], saved[1], saved[2], saved[3], saved[4])
    context, log_total, context_low, hidden, active = (
        saved[9],
        saved[10],
        saved[11],
        saved[12],
        saved[13],
    )
    row_count, model_width = stream_grad.shape
    head_size = model_width // head_count
    branch_grad = stream_grad.astype(jnp.bfloat16)
    branch_bias = jnp.sum(branch_grad.astype(jnp.float32), 0)
    out_grad = outer_sum(context_low, branch_grad)
    down_grad = outer_sum(active, branch_grad)
    context_grad = (
        against(branch_grad, w_out).astype(jnp.bfloat16).reshape(row_count, head_count, head_size)
    )
    active_grad = against(branch_grad, w_down)
    unused, gelu_pull = jax.vjp(gelu_exact, hidden)
    hidden_grad = gelu_pull(active_grad)[0].astype(jnp.bfloat16)
    up_grad = outer_sum(second, hidden_grad)
    up_bias_grad = jnp.sum(hidden_grad.astype(jnp.float32), 0)
    second_grad = against(hidden_grad, w_up)
    offsets = jnp.transpose(jnp.sum(context_grad.astype(jnp.float32) * context, -1), (1, 0))[
        :, :, None
    ]
    query_grad, key_grads, value_grads = attend_back(
        queries,
        keys_all,
        values_all,
        query_pos,
        key_pos,
        block_rows,
        log_total,
        offsets,
        context_grad,
    )
    key_grad, value_grad = (
        lax.psum_scatter(
            key_grads.astype(jnp.bfloat16), "ctx", scatter_dimension=0, tiled=True
        ).astype(jnp.float32),
        lax.psum_scatter(
            value_grads.astype(jnp.bfloat16), "ctx", scatter_dimension=0, tiled=True
        ).astype(jnp.float32),
    )
    query_raw = rope(query_grad, cosines, -sines).reshape(row_count, model_width)
    key_raw = rope(key_grad.reshape(row_count, head_count, head_size), cosines, -sines).reshape(
        row_count, model_width
    )
    mixed_grad = jnp.concatenate([query_raw, key_raw, value_grad], 1).astype(jnp.bfloat16)
    qkv_grad = outer_sum(first, mixed_grad)
    qkv_bias_grad = jnp.sum(mixed_grad.astype(jnp.float32), 0)
    first_grad = against(mixed_grad, w_qkv)
    gain_full = gain.astype(jnp.float32)
    normed_grad = first_grad * gain_full[0] + second_grad * gain_full[1]
    stream_back = stream_grad + inverse * (
        normed_grad
        - jnp.mean(normed_grad, -1, keepdims=True)
        - normed * jnp.mean(normed_grad * normed, -1, keepdims=True)
    )
    gain_grad = jnp.stack([jnp.sum(first_grad * normed, 0), jnp.sum(second_grad * normed, 0)])
    shift_grad = jnp.stack([jnp.sum(first_grad, 0), jnp.sum(second_grad, 0)])
    return (
        stream_back,
        (
            gain_grad,
            shift_grad,
            qkv_grad,
            qkv_bias_grad,
            out_grad,
            branch_bias,
            up_grad,
            up_bias_grad,
            down_grad,
            branch_bias,
        ),
    )


def on_device(
    hidden_in,
    cotangent,
    pair_table,
    norm_gain,
    norm_bias,
    qkv_weight,
    qkv_bias,
    out_weight,
    out_bias,
    up_weight,
    up_bias,
    down_weight,
    down_bias,
):
    row_count = hidden_in.shape[1]
    model_width = hidden_in.shape[2]
    slot_count = lax.axis_size("ctx")
    key_pos = pair_positions(pair_table, row_count // 2)
    query_pos = lax.dynamic_slice_in_dim(key_pos, lax.axis_index("ctx") * row_count, row_count)
    head_size = model_width // HEADS
    cosines, sines = rotation(query_pos, head_size // 4)
    group = 1
    while (
        group * 2 <= slot_count
        and slot_count % (group * 2) == 0
        and (row_count * group * 2 <= 1024)
    ):
        group = group * 2
    block_rows = row_count * group
    stream = hidden_in[0].astype(jnp.float32)
    layer_total = qkv_weight.shape[0]
    saved_list = []
    for layer_index in range(layer_total):
        gathered = (
            lax.all_gather(norm_gain[layer_index], "fsdp", axis=1, tiled=True),
            lax.all_gather(norm_bias[layer_index], "fsdp", axis=1, tiled=True),
            lax.all_gather(qkv_weight[layer_index], "fsdp", axis=0, tiled=True),
            lax.all_gather(qkv_bias[layer_index], "fsdp", axis=0, tiled=True),
            lax.all_gather(out_weight[layer_index], "fsdp", axis=0, tiled=True),
            lax.all_gather(out_bias[layer_index], "fsdp", axis=0, tiled=True),
            lax.all_gather(up_weight[layer_index], "fsdp", axis=0, tiled=True),
            lax.all_gather(up_bias[layer_index], "fsdp", axis=0, tiled=True),
            lax.all_gather(down_weight[layer_index], "fsdp", axis=0, tiled=True),
            lax.all_gather(down_bias[layer_index], "fsdp", axis=0, tiled=True),
        )
        stream, saved = layer_forward(
            stream, gathered, cosines, sines, query_pos, key_pos, block_rows, HEADS
        )
        saved_list.append(saved)
    output = stream.astype(jnp.bfloat16)[None]
    stream_grad = cotangent[0].astype(jnp.float32)
    collected = [None] * layer_total
    for layer_index in reversed(range(layer_total)):
        weights = (
            lax.all_gather(norm_gain[layer_index], "fsdp", axis=1, tiled=True),
            lax.all_gather(norm_bias[layer_index], "fsdp", axis=1, tiled=True),
            lax.all_gather(qkv_weight[layer_index], "fsdp", axis=0, tiled=True),
            lax.all_gather(qkv_bias[layer_index], "fsdp", axis=0, tiled=True),
            lax.all_gather(out_weight[layer_index], "fsdp", axis=0, tiled=True),
            lax.all_gather(out_bias[layer_index], "fsdp", axis=0, tiled=True),
            lax.all_gather(up_weight[layer_index], "fsdp", axis=0, tiled=True),
            lax.all_gather(up_bias[layer_index], "fsdp", axis=0, tiled=True),
            lax.all_gather(down_weight[layer_index], "fsdp", axis=0, tiled=True),
            lax.all_gather(down_bias[layer_index], "fsdp", axis=0, tiled=True),
        )
        saved = saved_list[layer_index]
        keys_all, values_all = (
            lax.all_gather(saved[5], "ctx", axis=0, tiled=True),
            lax.all_gather(saved[6], "ctx", axis=0, tiled=True),
        )
        stream_grad, grads = layer_backward(
            stream_grad,
            weights,
            saved,
            keys_all,
            values_all,
            cosines,
            sines,
            query_pos,
            key_pos,
            block_rows,
            HEADS,
        )
        shards = (
            lax.psum_scatter(
                grads[0].astype(jnp.bfloat16), "fsdp", scatter_dimension=1, tiled=True
            ).astype(jnp.float32),
            lax.psum_scatter(
                grads[1].astype(jnp.bfloat16), "fsdp", scatter_dimension=1, tiled=True
            ).astype(jnp.float32),
            lax.psum_scatter(
                grads[2].astype(jnp.bfloat16), "fsdp", scatter_dimension=0, tiled=True
            ).astype(jnp.float32),
            lax.psum_scatter(
                grads[3].astype(jnp.bfloat16), "fsdp", scatter_dimension=0, tiled=True
            ).astype(jnp.float32),
            lax.psum_scatter(
                grads[4].astype(jnp.bfloat16), "fsdp", scatter_dimension=0, tiled=True
            ).astype(jnp.float32),
            lax.psum_scatter(
                grads[5].astype(jnp.bfloat16), "fsdp", scatter_dimension=0, tiled=True
            ).astype(jnp.float32),
            lax.psum_scatter(
                grads[6].astype(jnp.bfloat16), "fsdp", scatter_dimension=0, tiled=True
            ).astype(jnp.float32),
            lax.psum_scatter(
                grads[7].astype(jnp.bfloat16), "fsdp", scatter_dimension=0, tiled=True
            ).astype(jnp.float32),
            lax.psum_scatter(
                grads[8].astype(jnp.bfloat16), "fsdp", scatter_dimension=0, tiled=True
            ).astype(jnp.float32),
            lax.psum_scatter(
                grads[9].astype(jnp.bfloat16), "fsdp", scatter_dimension=0, tiled=True
            ).astype(jnp.float32),
        )
        totals = (
            lax.psum(shards[0].astype(jnp.bfloat16), "ctx").astype(jnp.float32),
            lax.psum(shards[1].astype(jnp.bfloat16), "ctx").astype(jnp.float32),
            lax.psum(shards[2].astype(jnp.bfloat16), "ctx").astype(jnp.float32),
            lax.psum(shards[3].astype(jnp.bfloat16), "ctx").astype(jnp.float32),
            lax.psum(shards[4].astype(jnp.bfloat16), "ctx").astype(jnp.float32),
            lax.psum(shards[5].astype(jnp.bfloat16), "ctx").astype(jnp.float32),
            lax.psum(shards[6].astype(jnp.bfloat16), "ctx").astype(jnp.float32),
            lax.psum(shards[7].astype(jnp.bfloat16), "ctx").astype(jnp.float32),
            lax.psum(shards[8].astype(jnp.bfloat16), "ctx").astype(jnp.float32),
            lax.psum(shards[9].astype(jnp.bfloat16), "ctx").astype(jnp.float32),
        )
        collected[layer_index] = totals
    results = tuple(
        (
            jnp.stack([collected[layer_index][member] for layer_index in range(layer_total)])
            for member in range(10)
        )
    )
    return (
        output,
        stream_grad[None],
        results[0],
        results[1],
        results[2],
        results[3],
        results[4],
        results[5],
        results[6],
        results[7],
        results[8],
        results[9],
    )


def solution(mesh):
    placed = (
        P("fsdp", "ctx", None),
        P("fsdp", "ctx", None),
        P(),
        P(None, None, "fsdp"),
        P(None, None, "fsdp"),
        P(None, "fsdp", None),
        P(None, "fsdp"),
        P(None, "fsdp", None),
        P(None, "fsdp"),
        P(None, "fsdp", None),
        P(None, "fsdp"),
        P(None, "fsdp", None),
        P(None, "fsdp"),
    )
    return jax.shard_map(
        on_device,
        mesh=mesh,
        in_specs=placed,
        out_specs=(
            P("fsdp", "ctx", None),
            P("fsdp", "ctx", None),
            P(None, None, "fsdp"),
            P(None, None, "fsdp"),
            P(None, "fsdp", None),
            P(None, "fsdp"),
            P(None, "fsdp", None),
            P(None, "fsdp"),
            P(None, "fsdp", None),
            P(None, "fsdp"),
            P(None, "fsdp", None),
            P(None, "fsdp"),
        ),
        check_vma=False,
    )
```

profile of v0, /device:TPU:32, one launch (start us, length us, event | category | flops | bytes accessed | tf_op | source)
XLA Modules:
  0.0 3326.8 jit_solution(1618173531870269234)
XLA Ops:
  38.1 37.4 %all-gather.41.cloned.1.call-done = bf16[1,1024,3072]{2,1,0:T(8,128)(2,1)} async-done(((bf16[1,256,3072]{2,1,0:T(8,128)(2,1)}), bf16[1,1024,3072]{2,1,0:T(8,128)(2,1)}) %all-gather.41.cloned.1.call-update) | async-done | bytes 6291472 | tf_op jit(solution)/shard_map/all_gather | solution.py:338
  125.0 35.3 %all-gather.45.cloned.1.call-done = bf16[1,1024,4096]{2,1,0:T(8,128)(2,1)} async-done(((bf16[1,256,4096]{2,1,0:T(8,128)(2,1)}), bf16[1,1024,4096]{2,1,0:T(8,128)(2,1)}) %all-gather.45.cloned.1.call-update) | async-done | bytes 8388624 | tf_op jit(solution)/shard_map/all_gather | solution.py:342
  169.4 75.5 %all-gather.47.cloned.1.call-done = bf16[1,4096,1024]{2,1,0:T(8,128)(2,1)} async-done(((bf16[1,1024,1024]{2,1,0:T(8,128)(2,1)}), bf16[1,4096,1024]{2,1,0:T(8,128)(2,1)}) %all-gather.47.cloned.1.call-update) | async-done | bytes 8388624 | tf_op jit(solution)/shard_map/all_gather | solution.py:344
  249.6 142.4 %all-gather.33.cloned.1.call-done = bf16[4096,1024]{0,1:T(8,128)(2,1)} async-done(((bf16[128,1024]{0,1:T(8,128)(2,1)}), bf16[4096,1024]{0,1:T(8,128)(2,1)}) %all-gather.33.cloned.1.call-update) | async-done | bytes 8388624 | tf_op jit(solution)/shard_map/all_gather | solution.py:176
  416.2 82.5 %all-gather.35.cloned.1.call-done = bf16[4096,1024]{1,0:T(8,128)(2,1)} async-done(((bf16[128,1024]{1,0:T(8,128)(2,1)}), bf16[4096,1024]{1,0:T(8,128)(2,1)}) %all-gather.35.cloned.1.call-update) | async-done | bytes 8388624 | tf_op jit(solution)/shard_map/all_gather | solution.py:177
  539.2 69.1 %while.60 = (s32[]{:T(128)}, f32[16,128,1]{1,0,2:T(8,128)S(1)}, f32[16,128,1]{1,0,2:T(8,128)S(1)}, f32[16,128,64]{1,2,0:T(8,128)S(1)}, s32[4,1024]{1,0:T(4,128)S...) while((s32[]{:T(128)}, f32[16,128,1]{1,0,2:T(8,128)S(1)}, ...), condition=%wide.region_5.6_spmd.clone, body=%wide.region_2.5_spmd.clone.sunk | while | flops 564670464 | bytes 64893608 | solution.py:101
  627.9 144.4 %all-gather.37.cloned.1.call-done = bf16[4096,1024]{0,1:T(8,128)(2,1)} async-done(((bf16[128,1024]{0,1:T(8,128)(2,1)}), bf16[4096,1024]{0,1:T(8,128)(2,1)}) %all-gather.37.cloned.1.call-update) | async-done | bytes 8388624 | tf_op jit(solution)/shard_map/all_gather | solution.py:176
  796.6 83.0 %all-gather.39.cloned.1.call-done = bf16[4096,1024]{1,0:T(8,128)(2,1)} async-done(((bf16[128,1024]{1,0:T(8,128)(2,1)}), bf16[4096,1024]{1,0:T(8,128)(2,1)}) %all-gather.39.cloned.1.call-update) | async-done | bytes 8388624 | tf_op jit(solution)/shard_map/all_gather | solution.py:177
  920.2 69.5 %while.61 = (s32[]{:T(128)}, f32[16,128,1]{1,0,2:T(8,128)S(1)}, f32[16,128,1]{1,0,2:T(8,128)S(1)}, f32[16,128,64]{1,2,0:T(8,128)S(1)}, s32[4,1024]{1,0:T(4,128)S...) while((s32[]{:T(128)}, f32[16,128,1]{1,0,2:T(8,128)S(1)}, ...), condition=%wide.region_11.12_spmd.clone, body=%wide.region_8.11_spmd.clone.sunk | while | flops 564670464 | bytes 64893608 | solution.py:101
  998.7 94.7 %while.62 = (s32[]{:T(128)}, f32[128,16,64]{0,2,1:T(8,128)S(1)}, bf16[4,1024,16,64]{1,3,2,0:T(8,128)(2,1)}, bf16[4,1024,16,64]{1,3,2,0:T(8,128)(2,1)}, bf16[4,10...) while((s32[]{:T(128)}, f32[128,16,64]{0,2,1:T(8,128)S(1)}, ...), condition=%wide.region_14.15_spmd.clone, body=%wide.region_13.14_spmd.clone.sunk | while | flops 1364590592 | bytes 138842896 | solution.py:141
  1210.9 128.6 %reduce-scatter.49.cloned.1.call-done = bf16[128,1024]{1,0:T(8,128)(2,1)} async-done(((bf16[4096,1024]{1,0:T(8,128)(2,1)}), bf16[128,1024]{1,0:T(8,128)(2,1)}) %reduce-scatter.49.cloned.1.call-update) | async-done | bytes 262160
  1341.7 205.8 %reduce-scatter.51.cloned.1.call-done = bf16[128,1024]{1,0:T(8,128)(2,1)} async-done(((bf16[4096,1024]{1,0:T(8,128)(2,1)}), bf16[128,1024]{1,0:T(8,128)(2,1)}) %reduce-scatter.51.cloned.1.call-update) | async-done | bytes 262160
  1567.4 94.0 %while.63 = (s32[]{:T(128)}, f32[128,16,64]{0,2,1:T(8,128)S(1)}, bf16[4,1024,16,64]{1,3,2,0:T(8,128)(2,1)}, bf16[4,1024,16,64]{1,3,2,0:T(8,128)(2,1)}, bf16[4,10...) while((s32[]{:T(128)}, f32[128,16,64]{0,2,1:T(8,128)S(1)}, ...), condition=%wide.region_21.22_spmd.clone, body=%wide.region_20.21_spmd.clone.sunk | while | flops 1364590592 | bytes 138842896 | solution.py:141
  1794.3 114.1 %reduce-scatter.53.cloned.1.call-done = bf16[128,1024]{1,0:T(8,128)(2,1)} async-done(((bf16[4096,1024]{1,0:T(8,128)(2,1)}), bf16[128,1024]{1,0:T(8,128)(2,1)}) %reduce-scatter.53.cloned.1.call-update) | async-done | bytes 262160
  1909.6 206.1 %reduce-scatter.55.cloned.1.call-done = bf16[128,1024]{1,0:T(8,128)(2,1)} async-done(((bf16[4096,1024]{1,0:T(8,128)(2,1)}), bf16[128,1024]{1,0:T(8,128)(2,1)}) %reduce-scatter.55.cloned.1.call-update) | async-done | bytes 262160
  2139.6 54.8 %reduce-scatter.43.cloned.1.call-done = bf16[256,4096]{1,0:T(8,128)(2,1)} async-done(((bf16[1024,4096]{1,0:T(8,128)(2,1)}), bf16[256,4096]{1,0:T(8,128)(2,1)}) %reduce-scatter.43.cloned.1.call-update) | async-done | bytes 2097168 | tf_op jit(solution)/shard_map/reduce_scatter | solution.py:404
  2194.4 82.5 %reduce-scatter.47.cloned.1.call-done = bf16[1024,1024]{1,0:T(8,128)(2,1)} async-done(((bf16[4096,1024]{1,0:T(8,128)(2,1)}), bf16[1024,1024]{1,0:T(8,128)(2,1)}) %reduce-scatter.47.cloned.1.call-update) | async-done | bytes 2097168 | tf_op jit(solution)/shard_map/reduce_scatter | solution.py:410
  2276.9 31.7 reduce-scatter.39.cloned.1.call-done
  2340.2 66.6 %reduce-scatter.35.cloned.1.call-done = bf16[256,3072]{1,0:T(8,128)(2,1)} async-done(((bf16[1024,3072]{1,0:T(8,128)(2,1)}), bf16[256,3072]{1,0:T(8,128)(2,1)}) %reduce-scatter.35.cloned.1.call-update) | async-done | bytes 1572880 | tf_op jit(solution)/shard_map/reduce_scatter | solution.py:392
  2406.7 82.6 %reduce-scatter.41.cloned.1.call-done = bf16[256,4096]{1,0:T(8,128)(2,1)} async-done(((bf16[1024,4096]{1,0:T(8,128)(2,1)}), bf16[256,4096]{1,0:T(8,128)(2,1)}) %reduce-scatter.41.cloned.1.call-update) | async-done | bytes 2097168 | tf_op jit(solution)/shard_map/reduce_scatter | solution.py:404
  2489.3 82.6 %reduce-scatter.45.cloned.1.call-done = bf16[1024,1024]{1,0:T(8,128)(2,1)} async-done(((bf16[4096,1024]{1,0:T(8,128)(2,1)}), bf16[1024,1024]{1,0:T(8,128)(2,1)}) %reduce-scatter.45.cloned.1.call-update) | async-done | bytes 2097168 | tf_op jit(solution)/shard_map/reduce_scatter | solution.py:410
  2571.9 66.4 %reduce-scatter.33.cloned.1.call-done = bf16[256,3072]{1,0:T(8,128)(2,1)} async-done(((bf16[1024,3072]{1,0:T(8,128)(2,1)}), bf16[256,3072]{1,0:T(8,128)(2,1)}) %reduce-scatter.33.cloned.1.call-update) | async-done | bytes 1572880 | tf_op jit(solution)/shard_map/reduce_scatter | solution.py:392
  2723.2 185.1 %all-reduce.6 = (bf16[1,2,256]{2,1,0:T(2,128)(2,1)S(1)}, bf16[1,2,256]{2,1,0:T(2,128)(2,1)S(1)}, bf16[1,2,256]{2,1,0:T(2,128)(2,1)S(1)}, bf16[1,2,256]{2,1,0:T(2...) all-reduce(bf16[1,2,256]{2,1,0:T(2,128)(2,1)S(1)} %bitcast.647, ...), channel_id=1, replica_groups=mesh['ctx'=32,'fsdp'=4] {'ctx'}, use_global_device_ids=true, to_apply=%region_33.34 | all-reduce | flops 6144 | bytes 24576 | tf_op jit(solution)/shard_map/psum | solution.py:418
  2910.7 393.1 %all-reduce.11.cloned.1.call-done = (bf16[1,256,3072]{2,1,0:T(8,128)(2,1)}, bf16[1,256,3072]{2,1,0:T(8,128)(2,1)}, bf16[1,256,1024]{2,1,0:T(8,128)(2,1)}, bf16[1...) async-done(((bf16[1,256,3072]{2,1,0:T(8,128)(2,1)}, ...) | async-done | bytes 12582928 | tf_op jit(solution)/shard_map/psum | solution.py:420
  (651 shorter events, 1007.0 us)
Async XLA Ops:
  84.4 414.2 %all-gather.35.cloned.1.call-start = ((), (), s32[]{:S(2)}) async-start(), calls=%async_computation.17 | async-start | bytes 8650752 | tf_op jit(solution)/shard_map/all_gather | solution.py:177
  85.3 523.1 %all-gather.43.cloned.1.call-start = ((), (), s32[]{:S(2)}) async-start(), calls=%async_computation.29 | async-start | bytes 2621440 | tf_op jit(solution)/shard_map/all_gather | solution.py:340
  87.6 523.7 %all-gather.49.cloned.1.call-start = ((), (), s32[]{:S(2)}) async-start(), calls=%async_computation.32 | async-start | bytes 7864320 | tf_op jit(solution)/shard_map/all_gather | solution.py:338
  88.4 536.9 %all-gather.51.cloned.1.call-start = ((), (), s32[]{:S(2)}) async-start(), calls=%async_computation.33 | async-start | bytes 2621440 | tf_op jit(solution)/shard_map/all_gather | solution.py:340
  89.1 683.2 %all-gather.37.cloned.1.call-start = ((), (), s32[]{:S(2)}) async-start(), calls=%async_computation.18 | async-start | bytes 8650752 | tf_op jit(solution)/shard_map/all_gather | solution.py:176
  620.1 565.6 %all-gather.53.cloned.1.call-start = ((), (), s32[]{:S(2)}) async-start(), calls=%async_computation.34 | async-start | bytes 10485760 | tf_op jit(solution)/shard_map/all_gather | solution.py:342
  620.8 574.1 %all-gather.55.cloned.1.call-start = ((), (), s32[]{:S(2)}) async-start(), calls=%async_computation.35 | async-start | bytes 10485760 | tf_op jit(solution)/shard_map/all_gather | solution.py:344
  621.4 718.1 %reduce-scatter.49.cloned.1.call-start = ((), (), s32[]{:S(2)}) async-start(), calls=%async_computation.36 | async-start | bytes 8650752
  1136.3 411.2 %reduce-scatter.51.cloned.1.call-start = ((), (), s32[]{:S(2)}) async-start(), calls=%async_computation.37 | async-start | bytes 8650752
  1179.4 729.0 %reduce-scatter.53.cloned.1.call-start = ((), (), s32[]{:S(2)}) async-start(), calls=%async_computation.38 | async-start | bytes 8650752
  1704.3 411.4 %reduce-scatter.55.cloned.1.call-start = ((), (), s32[]{:S(2)}) async-start(), calls=%async_computation.39 | async-start | bytes 8650752
  1747.3 447.1 %reduce-scatter.43.cloned.1.call-start = ((), (), s32[]{:S(2)}) async-start(), calls=%async_computation.25 | async-start | bytes 10485760 | tf_op jit(solution)/shard_map/reduce_scatter | solution.py:404
  1754.8 522.0 %reduce-scatter.47.cloned.1.call-start = ((), (), s32[]{:S(2)}) async-start(), calls=%async_computation.27 | async-start | bytes 10485760 | tf_op jit(solution)/shard_map/reduce_scatter | solution.py:410
  1760.6 547.9 %reduce-scatter.39.cloned.1.call-start = ((), (), s32[]{:S(2)}) async-start(), calls=%async_computation.23 | async-start | bytes 2621440 | tf_op jit(solution)/shard_map/reduce_scatter | solution.py:398
  1763.8 576.4 %reduce-scatter.37.cloned.1.call-start = ((), (), s32[]{:S(2)}) async-start(), calls=%async_computation.22 | async-start | bytes 2621440 | tf_op jit(solution)/shard_map/reduce_scatter | solution.py:398
  1765.9 640.9 %reduce-scatter.35.cloned.1.call-start = ((), (), s32[]{:S(2)}) async-start(), calls=%async_computation.21 | async-start | bytes 7864320 | tf_op jit(solution)/shard_map/reduce_scatter | solution.py:392
  1770.6 718.7 %reduce-scatter.41.cloned.1.call-start = ((), (), s32[]{:S(2)}) async-start(), calls=%async_computation.24 | async-start | bytes 10485760 | tf_op jit(solution)/shard_map/reduce_scatter | solution.py:404
  1787.2 784.7 %reduce-scatter.45.cloned.1.call-start = ((), (), s32[]{:S(2)}) async-start(), calls=%async_computation.26 | async-start | bytes 10485760 | tf_op jit(solution)/shard_map/reduce_scatter | solution.py:410
  1794.1 844.2 %reduce-scatter.33.cloned.1.call-start = ((), (), s32[]{:S(2)}) async-start(), calls=%async_computation.20 | async-start | bytes 7864320 | tf_op jit(solution)/shard_map/reduce_scatter | solution.py:392
  2121.7 538.0 %reduce-scatter.59.cloned.1.call-start = ((), (), s32[]{:S(2)}) async-start(), calls=%async_computation.41 | async-start | bytes 327680
  2123.3 557.1 %reduce-scatter.63.cloned.1.call-start = ((), (), s32[]{:S(2)}) async-start(), calls=%async_computation.43 | async-start | bytes 327680
  2124.3 577.2 %reduce-scatter.57.cloned.1.call-start = ((), (), s32[]{:S(2)}) async-start(), calls=%async_computation.40 | async-start | bytes 327680
  2138.6 583.7 %reduce-scatter.61.cloned.1.call-start = ((), (), s32[]{:S(2)}) async-start(), calls=%async_computation.42 | async-start | bytes 327680
  2139.6 1164.2 %all-reduce.11.cloned.1.call-start = ((), (), s32[]{:S(2)}) async-start(), calls=%async_computation.44 | async-start | bytes 25165824 | tf_op jit(solution)/shard_map/psum | solution.py:420
  (132 other events, 7304.0 us)
Sparse Core Ops, SparseCore 0:
  11.1 64.2 all-gather.40
  77.7 82.5 all-gather.44
  162.6 82.3 all-gather.46
  248.1 143.8 all-gather.32
  394.9 103.7 all-gather.34
  528.0 64.7 all-gather.48
  595.0 30.1 all-gather.50
  628.6 143.7 all-gather.36
  775.8 103.7 all-gather.38
  881.2 78.2 all-gather.52
  961.0 82.3 all-gather.54
  1136.4 202.9 reduce-scatter.48
  1341.7 205.7 reduce-scatter.50
  1704.4 203.9 reduce-scatter.52
  1911.2 204.4 reduce-scatter.54
  2118.0 76.3 reduce-scatter.42
  2196.7 80.0 reduce-scatter.46
  2279.3 29.2 reduce-scatter.38
  2310.9 29.2 reduce-scatter.36
  2343.2 63.5 reduce-scatter.34
  2409.2 80.0 reduce-scatter.40
  2491.8 80.0 reduce-scatter.44
  2574.7 63.4 reduce-scatter.32
  2725.4 578.3 all-reduce.10
  (5 shorter events, 99.0 us)
where the time goes:
time: 3340 us; the launch traced here: 3330 us
  waiting for transfers between devices  2200 us (66%)
  matrix products  388 us (12%)
  local copies, waits for them, and re-layouts  386 us (12%)
  blocking collectives  260 us (8%)
  other arithmetic  71.1 us (2%)
    unnamed x37, waiting for transfers between devices  705 us
    psum x1, waiting for transfers between devices, on_device(): lax.psum(shards[2].astype(jnp.bfloat16), 'ctx').astype(jnp.float32)  393 us
    all_gather x2, waiting for transfers between devices, layer_forward(): lax.all_gather(keys_own, 'ctx', axis=0, tiled=True)  287 us
    unnamed x222, local copies, waits for them, and re-layouts  248 us
    psum x1, blocking collectives, on_device(): lax.psum(shards[0].astype(jnp.bfloat16), 'ctx').astype(jnp.float32)  185 us
    all_gather x2, waiting for transfers between devices, layer_forward(): lax.all_gather(values_own, 'ctx', axis=0, tiled=True)  165 us
    reduce_scatter x2, waiting for transfers between devices, on_device(): lax.psum_scatter(grads[8].astype(jnp.bfloat16), 'fsdp', scatter_dimension...  165 us
    reduce_scatter x2, waiting for transfers between devices, on_device(): lax.psum_scatter(grads[6].astype(jnp.bfloat16), 'fsdp', scatter_dimension...  137 us
  transfers between devices with their start and end apart: 29, of which 25 were waited for; matrix products, arithmetic and copies ran while one was open for 19% of the time, Pallas kernels for 0%

commit v1 on v0

v1 whole, which is shorter than its diff:
```python
import functools

import jax
import jax.numpy as jnp
from jax import lax
from jax.experimental import pallas as pl
from jax.experimental.pallas import tpu as pltpu
from jax.sharding import PartitionSpec as P

HEADS = 16
HEAD = 64
ROT = 16
BLK = 64
SIDE = 4
EPS = 1e-05
NEGATIVE = -1e30
MESH = pl.DeviceIdType.MESH
F32 = jnp.float32
BF16 = jnp.bfloat16
TILE = 256
KEYS = 512


def place():
    slot = lax.axis_index("ctx")
    return slot // 8, (slot // 2) % SIDE, slot % 2


def device(x, y, z):
    return {"ctx": ((x % SIDE) * SIDE + (y % SIDE)) * 2 + z}


class Grid:
    def __init__(self):
        self.x, self.y, self.z = place()

    def spot(self, half, dp, dq):
        dx, dy = (dp, dq) if half == 0 else (dq, dp)
        return (self.x + dx + SIDE) % SIDE, (self.y + dy + SIDE) % SIDE

    def rank(self, half, dp, dq):
        x, y = self.spot(half, dp, dq)
        return x * SIDE + y

    def device(self, half, dp, dq):
        x, y = self.spot(half, dp, dq)
        return device(x, y, self.z)

    def barrier(self):
        gate = pltpu.get_barrier_semaphore()
        for step in ((1, 0), (-1, 0), (0, 1), (0, -1)):
            pl.semaphore_signal(
                gate, inc=1, device_id=self.device(0, *step), device_id_type=MESH
            )
        pl.semaphore_wait(gate, 4)


def gather_plane(grid, own_ref, all_ref, send_sem, recv_sem, ready=None):
    rows = own_ref.shape[0]
    half_rows, quarter = rows // 2, rows // 4
    sends = []

    def view(half, dp, dq, low, count):
        return all_ref.at[grid.rank(half, dp, dq), pl.ds(half * half_rows + low, count)]

    def start(half, event, to, block, low, count, own=False):
        source = (
            own_ref.at[pl.ds(half * half_rows + low, count)]
            if own
            else view(half, *block, low, count)
        )
        copy = pltpu.make_async_remote_copy(
            src_ref=source,
            dst_ref=view(half, *block, low, count),
            send_sem=send_sem.at[half, event],
            recv_sem=recv_sem.at[half, event],
            device_id=grid.device(half, *to),
            device_id_type=MESH,
        )
        copy.start()
        sends.append(copy)

    def arrive(half, event, block, low, count):
        there = view(half, *block, low, count)
        pltpu.make_async_remote_copy(
            src_ref=there,
            dst_ref=there,
            send_sem=send_sem.at[half, event],
            recv_sem=recv_sem.at[half, event],
            device_id=grid.device(half, 1, 0),
            device_id_type=MESH,
        ).wait_recv()

    def spread(half, column, dp, own=False):
        start(half, 4 + 4 * column, (0, 1), (dp, 0), 0, half_rows, own)
        start(half, 5 + 4 * column, (0, -1), (dp, 0), 0, half_rows, own)

    for half in (0, 1):
        start(half, 0, (1, 0), (0, 0), 0, half_rows, True)
        start(half, 1, (-1, 0), (0, 0), 0, half_rows, True)
    for half in (0, 1):
        spread(half, 0, 0, True)
    for half in (0, 1):
        arrive(half, 0, (-1, 0), 0, half_rows)
        start(half, 2, (1, 0), (-1, 0), 0, quarter)
        spread(half, 1, -1)
    for half in (0, 1):
        arrive(half, 1, (1, 0), 0, half_rows)
        start(half, 3, (-1, 0), (1, 0), quarter, quarter)
        spread(half, 2, 1)
    for half in (0, 1):
        arrive(half, 2, (2, 0), 0, quarter)
        arrive(half, 3, (2, 0), quarter, quarter)
        spread(half, 3, 2)
    steps = (0, -1, 1, 2)
    for column in range(4):
        for half in (0, 1):
            arrive(half, 4 + 4 * column, (steps[column], -1), 0, half_rows)
            start(half, 6 + 4 * column, (0, 1), (steps[column], -1), 0, quarter)
            arrive(half, 5 + 4 * column, (steps[column], 1), 0, half_rows)
            start(half, 7 + 4 * column, (0, -1), (steps[column], 1), quarter, quarter)
    for column in range(4):
        for half in (0, 1):
            arrive(half, 6 + 4 * column, (steps[column], 2), 0, quarter)
            arrive(half, 7 + 4 * column, (steps[column], 2), quarter, quarter)
    for copy in sends:
        copy.wait_send()


def gather_kernel(own_ref, all_ref, local_sem, send_sem, recv_sem):
    grid = Grid()
    grid.barrier()
    keep = pltpu.make_async_copy(own_ref, all_ref.at[grid.rank(0, 0, 0)], local_sem)
    keep.start()
    gather_plane(grid, own_ref, all_ref, send_sem, recv_sem)
    keep.wait()


def plane_all_gather(own, name, number):
    return pl.pallas_call(
        gather_kernel,
        out_shape=jax.ShapeDtypeStruct((16,) + own.shape, own.dtype),
        in_specs=[pl.BlockSpec(memory_space=pl.ANY)],
        out_specs=pl.BlockSpec(memory_space=pl.ANY),
        scratch_shapes=[
            pltpu.SemaphoreType.DMA,
            pltpu.SemaphoreType.DMA((2, 20)),
            pltpu.SemaphoreType.DMA((2, 20)),
        ],
        name=name,
        compiler_params=pltpu.CompilerParams(collective_id=number, has_side_effects=True),
    )(own)


def scatter_plane(grid, part_ref, out_ref, land_half, land_full, stage, total, send_sem, recv_sem):
    rows = part_ref.shape[1]
    half_rows, quarter = rows // 2, rows // 4
    sends = []
    steps = (2, -1, 1, 0)

    def start(half, event, source, target, to):
        copy = pltpu.make_async_remote_copy(
            src_ref=source,
            dst_ref=target,
            send_sem=send_sem.at[half, event],
            recv_sem=recv_sem.at[half, event],
            device_id=grid.device(half, *to),
            device_id_type=MESH,
        )
        copy.start()
        sends.append(copy)

    def arrive(half, event, target):
        pltpu.make_async_remote_copy(
            src_ref=target,
            dst_ref=target,
            send_sem=send_sem.at[half, event],
            recv_sem=recv_sem.at[half, event],
            device_id=grid.device(half, 1, 0),
            device_id_type=MESH,
        ).wait_recv()

    def part(half, dp, dq, low=0, count=None):
        return part_ref.at[
            grid.rank(half, dp, dq),
            pl.ds(half * half_rows + low, half_rows if count is None else count),
        ]

    def move(phase):
        return (lambda s: (0, s)) if phase == 0 else (lambda s: (s, 0))

    def opposite(half, column, pieces, step):
        start(
            half, 4 * column, pieces(2, 0, quarter), land_half.at[half, column, 0], step(1)
        )
        start(
            half,
            4 * column + 1,
            pieces(2, quarter, quarter),
            land_half.at[half, column, 1],
            step(-1),
        )

    def neighbours(half, column, pieces, step):
        arrive(half, 4 * column, land_half.at[half, column, 0])
        stage[half, column, 0, 0:quarter] = (
            pieces(1, 0, quarter)[...].astype(F32)
            + land_half[half, column, 0].astype(F32)
        ).astype(BF16)
        stage[half, column, 0, quarter:half_rows] = pieces(1, quarter, quarter)[...]
        start(
            half, 4 * column + 2, stage.at[half, column, 0], land_full.at[half, column, 0], step(1)
        )
        arrive(half, 4 * column + 1, land_half.at[half, column, 1])
        stage[half, column, 1, 0:quarter] = pieces(-1, 0, quarter)[...]
        stage[half, column, 1, quarter:half_rows] = (
            pieces(-1, quarter, quarter)[...].astype(F32)
            + land_half[half, column, 1].astype(F32)
        ).astype(BF16)
        start(
            half, 4 * column + 3, stage.at[half, column, 1], land_full.at[half, column, 1], step(-1)
        )

    def settle(half, column, own):
        arrive(half, 4 * column + 2, land_full.at[half, column, 0])
        arrive(half, 4 * column + 3, land_full.at[half, column, 1])
        return (
            own[...].astype(F32)
            + land_full[half, column, 0].astype(F32)
            + land_full[half, column, 1].astype(F32)
        )

    def first(column):
        dp = steps[column]
        return lambda half: (
            lambda dq, low, count: part(half, dp, dq, low, count)
        )

    second_index = {2: 0, -1: 1, 1: 2, 0: 3}

    def second(half):
        return lambda dp, low, count: total.at[half, second_index[dp], pl.ds(low, count)]

    along, across = move(0), move(1)
    for column in range(4):
        for half in (0, 1):
            opposite(half, column, first(column)(half), along)
    for column in range(4):
        for half in (0, 1):
            neighbours(half, column, first(column)(half), along)
    for column in range(4):
        for half in (0, 1):
            total[half, column] = settle(half, column, part(half, steps[column], 0)).astype(BF16)
            if column == 0:
                opposite(half, 4, second(half), across)
            if column == 2:
                neighbours(half, 4, second(half), across)
    for half in (0, 1):
        out_ref[pl.ds(half * half_rows, half_rows)] = settle(half, 4, total.at[half, 3])
    for copy in sends:
        copy.wait_send()


def scatter_kernel(part_ref, out_ref, land_half, land_full, stage, total, send_sem, recv_sem):
    grid = Grid()
    grid.barrier()
    scatter_plane(
        grid, part_ref, out_ref, land_half, land_full, stage, total, send_sem, recv_sem
    )


def plane_reduce_scatter(part, name, number):
    ranks, rows, width = part.shape
    half_rows, quarter = rows // 2, rows // 4
    return pl.pallas_call(
        scatter_kernel,
        out_shape=jax.ShapeDtypeStruct((rows, width), F32),
        in_specs=[pl.BlockSpec(memory_space=pltpu.VMEM)],
        out_specs=pl.BlockSpec(memory_space=pltpu.VMEM),
        scratch_shapes=[
            pltpu.VMEM((2, 5, 2, quarter, width), BF16),
            pltpu.VMEM((2, 5, 2, half_rows, width), BF16),
            pltpu.VMEM((2, 5, 2, half_rows, width), BF16),
            pltpu.VMEM((2, 4, half_rows, width), BF16),
            pltpu.SemaphoreType.DMA((2, 20)),
            pltpu.SemaphoreType.DMA((2, 20)),
        ],
        name=name,
        compiler_params=pltpu.CompilerParams(
            collective_id=number, has_side_effects=True, vmem_limit_bytes=40 << 20
        ),
    )(part)


def dots(a, b, da, db):
    return lax.dot_general(a, b, (((da,), (db,)), ((), ())), preferred_element_type=F32)


def sort_in(source_ref, order_ref, target_ref, count):
    def body(i, unused):
        start = pl.multiple_of(order_ref[i] * BLK, BLK)
        target_ref[pl.ds(pl.multiple_of(i * BLK, BLK), BLK), :] = source_ref[
            pl.ds(start, BLK), :
        ]
        return unused

    lax.fori_loop(0, count, body, 0)


def tile_positions(number_ref, tile, axis):
    per = TILE // BLK
    shape = (TILE, 1) if axis == 0 else (1, TILE)
    row = lax.broadcasted_iota(jnp.int32, shape, axis)
    base = jnp.zeros(shape, jnp.int32)
    for i in range(per):
        base = jnp.where(row // BLK == i, number_ref[tile * per + i] * BLK, base)
    return base + row % BLK


def attend_kernel(
    source_ref, order_ref, number_ref, q_ref, kv_ref, context_ref, log_ref, qs, kvs
):
    sort_in(kv_ref, source_ref, kvs, 64)
    sort_in(q_ref, order_ref, qs, 32)
    per = TILE // BLK

    def one_tile(tile, unused):
        queries = qs[pl.ds(pl.multiple_of(tile * TILE, TILE), TILE), :]
        low = number_ref[tile * per] * BLK
        high = (number_ref[tile * per + per - 1] + 1) * BLK
        positions = tile_positions(number_ref, tile, 0)

        def step(masked):
            def body(index, carry):
                row_max, row_sum, weighted = carry
                keys = kvs[pl.ds(pl.multiple_of(index * KEYS, KEYS), KEYS), :]
                scores = dots(queries, keys, 1, 1)
                if masked:
                    spots = index * KEYS + lax.broadcasted_iota(jnp.int32, (1, KEYS), 1)
                    scores = jnp.where(spots <= positions, scores, NEGATIVE)
                new_max = jnp.maximum(row_max, jnp.max(scores, 1, keepdims=True))
                weights = jnp.exp(scores - new_max)
                rescale = jnp.exp(row_max - new_max)
                row_sum = row_sum * rescale + jnp.sum(weights, 1, keepdims=True)
                weighted = weighted * rescale + dots(weights.astype(BF16), keys, 1, 0)
                return new_max, row_sum, weighted

            return body

        carry = (
            jnp.full((TILE, 1), NEGATIVE, F32),
            jnp.zeros((TILE, 1), F32),
            jnp.zeros((TILE, 2 * HEAD), F32),
        )
        clear = (low + 1) // KEYS
        carry = lax.fori_loop(0, clear, step(False), carry)
        row_max, row_sum, weighted = lax.fori_loop(
            clear, (high + KEYS - 1) // KEYS, step(True), carry
        )
        result = weighted / row_sum
        logs = jnp.broadcast_to(row_max + jnp.log(row_sum), (TILE, 2 * HEAD))
        for i in range(per):
            start = pl.multiple_of(order_ref[tile * per + i] * BLK, BLK)
            context_ref[pl.ds(start, BLK), :] = result[i * BLK : (i + 1) * BLK]
            log_ref[pl.ds(start, BLK), :] = logs[i * BLK : (i + 1) * BLK]
        return unused

    lax.fori_loop(0, 2048 // TILE, one_tile, 0)


def attend(source, order, number, queries, pairs):
    rows = queries.shape[0]
    smem, vmem = pl.BlockSpec(memory_space=pltpu.SMEM), pl.BlockSpec(memory_space=pltpu.VMEM)
    return pl.pallas_call(
        attend_kernel,
        out_shape=[
            jax.ShapeDtypeStruct((rows, 2 * HEAD), F32),
            jax.ShapeDtypeStruct((rows, 2 * HEAD), F32),
        ],
        in_specs=[smem, smem, smem, vmem, vmem],
        out_specs=[vmem, vmem],
        scratch_shapes=[
            pltpu.VMEM((rows, 2 * HEAD), BF16),
            pltpu.VMEM(pairs.shape, BF16),
        ],
        name="attend",
        compiler_params=pltpu.CompilerParams(vmem_limit_bytes=40 << 20),
    )(source, order, number, queries, pairs)


def attend_back_kernel(
    source_ref,
    order_ref,
    number_ref,
    q_ref,
    kv_ref,
    pull_ref,
    stat_ref,
    query_grad_ref,
    pair_grad_ref,
    qs,
    kvs,
    pulls,
    stats,
    sums,
):
    sort_in(kv_ref, source_ref, kvs, 64)
    sort_in(q_ref, order_ref, qs, 32)
    sort_in(pull_ref, order_ref, pulls, 32)
    sort_in(stat_ref, order_ref, stats, 32)
    sums[...] = jnp.zeros_like(sums)
    per = TILE // BLK

    def one_tile(tile, unused):
        rows = pl.ds(pl.multiple_of(tile * TILE, TILE), TILE)
        queries, pull = qs[rows, :], pulls[rows, :]
        turned = jnp.transpose(stats[rows, :])
        log_total, offset = turned[0:1, :], turned[1:2, :]
        low = number_ref[tile * per] * BLK
        high = (number_ref[tile * per + per - 1] + 1) * BLK
        positions = tile_positions(number_ref, tile, 1)

        def step(masked):
            def body(index, query_grad):
                spot = pl.ds(pl.multiple_of(index * KEYS, KEYS), KEYS)
                keys = kvs[spot, :]
                scores = dots(keys, queries, 1, 1)
                if masked:
                    spots = index * KEYS + lax.broadcasted_iota(jnp.int32, (KEYS, 1), 0)
                    scores = jnp.where(spots <= positions, scores, NEGATIVE)
                probs = jnp.exp(scores - log_total)
                prob_grad = dots(keys, pull, 1, 1)
                score_grad = (probs * (prob_grad - offset)).astype(BF16)
                sums[spot, :] += dots(score_grad, queries, 1, 0) + dots(
                    probs.astype(BF16), pull, 1, 0
                )
                return query_grad + dots(score_grad, keys, 0, 0)

            return body

        clear = (low + 1) // KEYS
        carry = jnp.zeros((TILE, 2 * HEAD), F32)
        carry = lax.fori_loop(0, clear, step(False), carry)
        carry = lax.fori_loop(clear, (high + KEYS - 1) // KEYS, step(True), carry)
        for i in range(per):
            start = pl.multiple_of(order_ref[tile * per + i] * BLK, BLK)
            query_grad_ref[pl.ds(start, BLK), :] = carry[i * BLK : (i + 1) * BLK]
        return unused

    lax.fori_loop(0, 2048 // TILE, one_tile, 0)

    def put(i, unused):
        start = pl.multiple_of(source_ref[i] * BLK, BLK)
        pair_grad_ref[pl.ds(start, BLK), :] = sums[
            pl.ds(pl.multiple_of(i * BLK, BLK), BLK), :
        ].astype(BF16)
        return unused

    lax.fori_loop(0, 64, put, 0)


def attend_back(source, order, number, queries, pairs, pull, stats):
    rows = queries.shape[0]
    smem, vmem = pl.BlockSpec(memory_space=pltpu.SMEM), pl.BlockSpec(memory_space=pltpu.VMEM)
    return pl.pallas_call(
        attend_back_kernel,
        out_shape=[
            jax.ShapeDtypeStruct((rows, 2 * HEAD), F32),
            jax.ShapeDtypeStruct(pairs.shape, BF16),
        ],
        in_specs=[smem, smem, smem, vmem, vmem, vmem, vmem],
        out_specs=[vmem, vmem],
        scratch_shapes=[
            pltpu.VMEM((rows, 2 * HEAD), BF16),
            pltpu.VMEM(pairs.shape, BF16),
            pltpu.VMEM((rows, 2 * HEAD), BF16),
            pltpu.VMEM((rows, 2 * HEAD), F32),
            pltpu.VMEM(pairs.shape, F32),
        ],
        name="attend_back",
        compiler_params=pltpu.CompilerParams(vmem_limit_bytes=48 << 20),
    )(source, order, number, queries, pairs, pull, stats)


def block_tables(pair_table, z):
    slots = pair_table.shape[0]
    ranks = slots // 2
    own = lax.dynamic_slice_in_dim(pair_table.reshape(ranks, 2), z, 1, 1)
    numbers = jnp.concatenate([own, 2 * slots - 1 - own], 1).reshape(-1)
    index = jnp.arange(slots, dtype=jnp.int32)
    standing = jnp.sum((numbers[None, :] < numbers[:, None]).astype(jnp.int32), 1)
    chosen = (standing[None, :] == index[:, None]).astype(jnp.int32)
    order = jnp.sum(chosen * index[None, :], 1)
    sorted_numbers = jnp.sum(chosen * numbers[None, :], 1)
    slot_of = jnp.sum(
        (pair_table[None, :] == index[:, None]).astype(jnp.int32) * index[None, :], 1
    )
    lies = jnp.where(slot_of % 2 == z, 0, slots) + (slot_of // 2) * 2
    source = jnp.concatenate([lies, lies[::-1] + 1])
    return numbers, order, sorted_numbers, source


def rotation(positions):
    freqs = 10000.0 ** (-jnp.arange(0, ROT, 2, dtype=F32) / ROT)
    angles = positions.astype(F32)[:, None] * freqs[None, :]
    return (jnp.concatenate([jnp.cos(angles)] * 2, -1), jnp.concatenate([jnp.sin(angles)] * 2, -1))


def rope(inputs, cosines, sines):
    half_dims = ROT // 2
    turning = inputs[..., :ROT]
    turned = jnp.concatenate([-turning[..., half_dims:], turning[..., :half_dims]], -1)
    return jnp.concatenate([turning * cosines + turned * sines, inputs[..., ROT:]], -1)


def standardize(stream):
    row_mean = jnp.mean(stream, -1, keepdims=True)
    centered = stream - row_mean
    spread = jnp.mean(centered * centered, -1, keepdims=True)
    inverse = lax.rsqrt(spread + EPS)
    return (centered * inverse, inverse)


def gelu_exact(inputs):
    return jax.nn.gelu(inputs, approximate=False)


def swap(value):
    pairs = [(i, i ^ 1) for i in range(lax.axis_size("ctx"))]
    return lax.ppermute(value, "ctx", pairs)


def on_device(
    hidden_in,
    cotangent,
    pair_table,
    norm_gain,
    norm_bias,
    qkv_weight,
    qkv_bias,
    out_weight,
    out_bias,
    up_weight,
    up_bias,
    down_weight,
    down_bias,
):
    layers = norm_gain.shape[0]
    slot = lax.axis_index("ctx")
    shard = lax.axis_index("fsdp")
    rank, z = slot // 2, slot % 2
    width = hidden_in.shape[2]
    quarter = width // 4

    numbers, order, sorted_numbers, source = block_tables(pair_table, z)
    positions = (
        numbers[:, None] * BLK + jnp.arange(BLK, dtype=jnp.int32)[None, :]
    ).reshape(-1)
    cosines, sines = rotation(positions)

    pieces = [
        lax.dynamic_slice_in_dim(qkv_weight, part * width + rank * HEAD, HEAD, 2)
        for part in range(3)
    ] + [
        lax.dynamic_slice_in_dim(up_weight, part * width + rank * HEAD, HEAD, 2)
        for part in range(4)
    ]
    wide = lax.all_gather(jnp.concatenate(pieces, 2), "fsdp", axis=1, tiled=True)
    tall = lax.all_gather(
        jnp.concatenate(
            [
                lax.dynamic_slice_in_dim(down_weight, rank * HEAD, HEAD, 1),
                lax.dynamic_slice_in_dim(out_weight, (rank % 4) * HEAD, HEAD, 1),
            ],
            1,
        ),
        "fsdp",
        axis=0,
    )
    vectors = lax.all_gather(
        jnp.concatenate(
            [
                norm_gain.reshape(layers, -1),
                norm_bias.reshape(layers, -1),
                qkv_bias,
                out_bias,
                up_bias,
                down_bias,
            ],
            1,
        ),
        "fsdp",
        axis=0,
    ).astype(F32)
    out_all = lax.dynamic_slice_in_dim(tall, rank // 4, 1, 0)[0, :, HEAD:]

    weights = []
    for layer in range(layers):
        vector = vectors[:, layer]
        gain = jnp.transpose(vector[:, 0:512].reshape(4, 2, 256), (1, 0, 2)).reshape(2, width)
        shift = jnp.transpose(vector[:, 512:1024].reshape(4, 2, 256), (1, 0, 2)).reshape(2, width)
        b_qkv = lax.dynamic_slice_in_dim(
            vector[:, 1024:1792].reshape(3, 16, HEAD), rank, 1, 1
        ).reshape(3 * HEAD)
        b_out = vector[:, 1792:2048].reshape(width)
        b_up = lax.dynamic_slice_in_dim(
            vector[:, 2048:3072].reshape(4, 16, HEAD), rank, 1, 1
        ).reshape(4 * HEAD)
        b_down = vector[:, 3072:3328].reshape(width)
        weights.append(
            (
                gain,
                shift,
                wide[layer, :, : 3 * HEAD],
                b_qkv,
                out_all[layer],
                wide[layer, :, 3 * HEAD :],
                b_up,
                tall[:, layer, :HEAD].reshape(4 * HEAD, width),
                b_out + b_down,
            )
        )

    number = 1
    stream = hidden_in[0].astype(F32)
    saved = []
    for layer in range(layers):
        gain, shift, w_qkv, b_qkv, w_out, w_up, b_up, w_down, b_last = weights[layer]
        normed, inverse = standardize(stream)
        normed_all = plane_all_gather(normed.astype(BF16), "gather_normed", number).reshape(
            -1, width
        )
        number += 1
        plain = normed_all.astype(F32)
        first = (plain * gain[0] + shift[0]).astype(BF16)
        second = (plain * gain[1] + shift[1]).astype(BF16)
        mixed = jnp.dot(first, w_qkv, preferred_element_type=F32) + b_qkv
        q = rope(mixed[:, :HEAD], cosines, sines).astype(BF16)
        k = rope(mixed[:, HEAD : 2 * HEAD], cosines, sines).astype(BF16)
        v = mixed[:, 2 * HEAD :].astype(BF16)
        queries = jnp.concatenate([q * jnp.asarray(0.125, BF16), jnp.zeros_like(q)], 1)
        pairs = jnp.concatenate([k, v], 1)
        pairs = jnp.concatenate([pairs, swap(pairs)], 0)
        context, logs = attend(source, order, sorted_numbers, queries, pairs)
        context_low = context[:, HEAD:].astype(BF16)
        hidden = jnp.dot(second, w_up, preferred_element_type=F32) + b_up
        active = gelu_exact(hidden).astype(BF16)
        partial = (
            jnp.dot(context_low, w_out, preferred_element_type=F32)
            + jnp.dot(active, w_down, preferred_element_type=F32)
        ).astype(BF16)
        summed = plane_reduce_scatter(partial.reshape(16, -1, width), "scatter_out", number)
        number += 1
        stream = stream + summed + b_last
        saved.append(
            (normed, inverse, normed_all, queries, pairs, context, logs, context_low, hidden, active)
        )
    output = stream.astype(BF16)[None]

    grad = cotangent[0].astype(F32)
    grads = [None] * layers
    for layer in reversed(range(layers)):
        gain, shift, w_qkv, b_qkv, w_out, w_up, b_up, w_down, b_last = weights[layer]
        normed, inverse, normed_all, queries, pairs, context, logs, context_low, hidden, active = (
            saved[layer]
        )
        branch = grad.astype(BF16)
        branch_bias = jnp.sum(branch.astype(F32), 0)
        branch_all = plane_all_gather(branch, "gather_branch", number).reshape(-1, width)
        number += 1
        out_grad = dots(context_low, branch_all, 0, 0)
        down_grad = dots(active, branch_all, 0, 0)
        context_grad = dots(branch_all, w_out, 1, 1).astype(BF16)
        active_grad = dots(branch_all, w_down, 1, 1)
        unused, gelu_pull = jax.vjp(gelu_exact, hidden)
        hidden_grad = gelu_pull(active_grad)[0].astype(BF16)
        up_raw = dots(normed_all, hidden_grad, 0, 0)
        up_bias_grad = jnp.sum(hidden_grad.astype(F32), 0)
        offsets = jnp.sum(context_grad.astype(F32) * context[:, HEAD:], 1, keepdims=True)
        lane = lax.broadcasted_iota(jnp.int32, (1, 2 * HEAD), 1)
        stats = jnp.where(lane == 0, logs, offsets)
        pull = jnp.concatenate([jnp.zeros_like(context_grad), context_grad], 1)
        query_grad, pair_grads = attend_back(
            source, order, sorted_numbers, queries, pairs, pull, stats
        )
        own_rows = queries.shape[0]
        pair_grad = pair_grads[:own_rows].astype(F32) + swap(pair_grads[own_rows:]).astype(F32)
        mixed_grad = jnp.concatenate(
            [
                rope(query_grad[:, :HEAD] * 0.125, cosines, -sines),
                rope(pair_grad[:, :HEAD], cosines, -sines),
                pair_grad[:, HEAD:],
            ],
            1,
        ).astype(BF16)
        qkv_raw = dots(normed_all, mixed_grad, 0, 0)
        qkv_bias_grad = jnp.sum(mixed_grad.astype(F32), 0)
        first_grad = dots(mixed_grad, w_qkv, 1, 1)
        second_grad = dots(hidden_grad, w_up, 1, 1)
        partial = (first_grad * gain[0] + second_grad * gain[1]).astype(BF16)
        normed_grad = plane_reduce_scatter(
            partial.reshape(16, -1, width), "scatter_normed", number
        )
        number += 1
        grad = grad + inverse * (
            normed_grad
            - jnp.mean(normed_grad, -1, keepdims=True)
            - normed * jnp.mean(normed_grad * normed, -1, keepdims=True)
        )
        full_qkv, full_up = w_qkv.astype(F32), w_up.astype(F32)
        vector_parts = jnp.stack(
            [
                jnp.sum(full_qkv * qkv_raw, 1),
                jnp.sum(full_up * up_raw, 1),
                jnp.sum(full_qkv * qkv_bias_grad, 1),
                jnp.sum(full_up * up_bias_grad, 1),
                branch_bias,
            ]
        )
        qkv_grad = qkv_raw * gain[0][:, None] + shift[0][:, None] * qkv_bias_grad
        up_grad = up_raw * gain[1][:, None] + shift[1][:, None] * up_bias_grad
        grads[layer] = (
            jnp.concatenate([qkv_grad, up_grad], 1),
            down_grad,
            out_grad,
            vector_parts,
            qkv_bias_grad,
            up_bias_grad,
        )

    wide_grad, down_grad, out_grad, vector_grad, qkv_bias_grad, up_bias_grad = (
        jnp.stack([grads[layer][i] for layer in range(layers)]) for i in range(6)
    )
    wide_grad = lax.psum_scatter(
        wide_grad.astype(BF16), "fsdp", scatter_dimension=1, tiled=True
    )
    down_grad = lax.psum_scatter(
        down_grad.astype(BF16), "fsdp", scatter_dimension=1, tiled=True
    )
    out_grad = lax.psum(out_grad.astype(BF16), "fsdp")
    tall_grad = jnp.concatenate([down_grad, out_grad], 1)
    wide_grad = (wide_grad.astype(F32) + swap(wide_grad).astype(F32)).astype(BF16)
    tall_grad = (tall_grad.astype(F32) + swap(tall_grad).astype(F32)).astype(BF16)
    wide_all = plane_all_gather(wide_grad.reshape(-1, 7 * HEAD), "gather_wide", number)
    number += 1
    tall_all = plane_all_gather(tall_grad.reshape(-1, width), "gather_tall", number)
    number += 1
    wide_all = wide_all.reshape(16, layers, quarter, 7, HEAD)
    wide_all = jnp.transpose(wide_all, (1, 2, 3, 0, 4)).reshape(layers, quarter, 7 * width)
    qkv_out = wide_all[:, :, : 3 * width].astype(F32)
    up_out = wide_all[:, :, 3 * width :].astype(F32)
    tall_all = tall_all.reshape(16, layers, 2, HEAD, width)
    tall_all = tall_all.astype(F32)
    down_out = jnp.transpose(tall_all[:, :, 0], (1, 0, 2, 3)).reshape(layers, width, width)
    out_out = jnp.transpose(
        lax.dynamic_slice_in_dim(tall_all[:, :, 1], shard * 4, 4, 0), (1, 0, 2, 3)
    ).reshape(layers, quarter, width)

    zeros = jnp.zeros((layers, 7, 16, HEAD), F32)
    biases = jnp.concatenate([qkv_bias_grad, up_bias_grad], 1).reshape(layers, 7, 1, HEAD)
    biases = lax.dynamic_update_slice_in_dim(zeros, biases, rank, 2).reshape(layers, -1)
    small = lax.psum(
        jnp.concatenate([vector_grad.reshape(layers, -1), biases], 1), ("ctx", "fsdp")
    )

    def mine(start, total):
        share = total // 4
        return lax.dynamic_slice_in_dim(small, start + shard * share, share, 1)

    gain_out = jnp.stack([mine(0, width), mine(width, width)], 1)
    shift_out = jnp.stack([mine(2 * width, width), mine(3 * width, width)], 1)
    branch_out = mine(4 * width, width)
    qkv_bias_out = mine(5 * width, 3 * width)
    up_bias_out = mine(8 * width, 4 * width)
    return (
        output,
        grad[None],
        gain_out,
        shift_out,
        qkv_out,
        qkv_bias_out,
        out_out,
        branch_out,
        up_out,
        up_bias_out,
        down_out,
        branch_out,
    )


def solution(mesh):
    rows = P("fsdp", "ctx", None)
    vector, matrix = P(None, "fsdp"), P(None, "fsdp", None)
    gains = P(None, None, "fsdp")
    params = (gains, gains) + (matrix, vector) * 4
    return jax.shard_map(
        on_device,
        mesh=mesh,
        in_specs=(rows, rows, P()) + params,
        out_specs=(rows, rows) + params,
        check_vma=False,
    )
```

time: 3340 us -> 772 us (0.23)
  waiting for transfers between devices: 2200 us -> 127 us
  Pallas kernels: 0 us -> 380 us
  matrix products: 388 us -> 69.3 us
  local copies, waits for them, and re-layouts: 386 us -> 90.3 us
  blocking collectives: 260 us -> 5.24 us
    unnamed x37 -> x6, waiting for transfers between devices: 705 us -> 0.1 us
    all_gather x12 -> x2, waiting for transfers between devices: 604 us -> 0.01 us  [the longest x1 0.01 us: on_device(): lax.all_gather(jnp.concatenate(pieces, 2), 'fsdp', axis=1, tiled=True)]
    reduce_scatter x8 -> x2, waiting for transfers between devices: 499 us -> 0.01 us  [the longest x1 0.01 us: on_device(): lax.psum_scatter(down_grad.astype(BF16), 'fsdp', scatter_dimension=1, til...]
    pallas_call x0 -> x14, Pallas kernels: none -> 380 us  [the longest x6 200 us: plane_all_gather(): pl.pallas_call(gather_kernel, out_shape=jax.ShapeDtypeStruct((16,) + own....]
    dot_general x80 -> x24, matrix products: 388 us -> 69.3 us  [the longest x16 43.4 us: dots(): lax.dot_general(a, b, (((da,), (db,)), ((), ())), preferred_element_type=...]
    psum x1 -> x2, waiting for transfers between devices: 393 us -> 125 us  [the longest x1 125 us: on_device(): lax.psum(jnp.concatenate([vector_grad.reshape(layers, -1), biases], 1), (...]
    unnamed x222 -> x205, local copies, waits for them, and re-layouts: 248 us -> 27.4 us
    psum x1 -> x0, blocking collectives: 185 us -> none  [on_device(): lax.psum(shards[0].astype(jnp.bfloat16), 'ctx').astype(jnp.float32)]
  transfers between devices with their start and end apart: 29 -> 12, of which waited for: 25 -> 2; matrix products, arithmetic and copies ran while one was open for 19% -> 16% of each run, Pallas kernels for 0% -> 22%
where the time goes in v1:
time: 772 us; the launch traced here: 761 us
  Pallas kernels  380 us (49%)
  waiting for transfers between devices  127 us (16%)
  local copies, waits for them, and re-layouts  90.3 us (12%)
  matrix products  69.3 us (9%)
  other arithmetic  61 us (8%)
  between operations  16.4 us (2%)
  starting transfers between devices  12 us (2%)
    pallas_call x6, Pallas kernels, plane_all_gather(): pl.pallas_call(gather_kernel, out_shape=jax.ShapeDtypeStruct((16,) + own....  200 us
    psum x1, waiting for transfers between devices, on_device(): lax.psum(jnp.concatenate([vector_grad.reshape(layers, -1), biases], 1), (...  125 us
    pallas_call x4, Pallas kernels, plane_reduce_scatter(): pl.pallas_call(scatter_kernel, out_shape=jax.ShapeDtypeStruct((rows, widt...  93.2 us
    pallas_call x2, Pallas kernels, attend_back(): pl.pallas_call(attend_back_kernel, out_shape=[jax.ShapeDtypeStruct((rows,...  46.1 us
    dot_general x16, matrix products, dots(): lax.dot_general(a, b, (((da,), (db,)), ((), ())), preferred_element_type=...  43.4 us
    pallas_call x2, Pallas kernels, attend(): pl.pallas_call(attend_kernel, out_shape=[jax.ShapeDtypeStruct((rows, 2 *...  40.3 us
    unnamed x205, local copies, waits for them, and re-layouts  27.4 us
  transfers between devices with their start and end apart: 12, of which 2 were waited for; matrix products, arithmetic and copies ran while one was open for 16% of the time, Pallas kernels for 22%

profile of v1, /device:TPU:32, one launch (start us, length us, event | category | flops | bytes accessed | tf_op | source)
XLA Modules:
  0.0 760.5 jit_solution(7220796705942192776)
XLA Ops:
  24.8 29.9 %gather_normed.2 = bf16[16,128,1024]{2,1,0:T(8,128)(2,1)} custom-call(bf16[128,1024]{1,0:T(8,128)(2,1)} %fusion.54.own_ref), custom_call_target="tpu_custom_call" | custom-call | tf_op jit(solution)/shard_map/gather_normed/pallas_call | solution.py:140
  54.7 27.1 %gather_branch.2 = bf16[16,128,1024]{2,1,0:T(8,128)(2,1)} custom-call(bf16[128,1024]{1,0:T(8,128)(2,1)} %bitcast.271), custom_call_target="tpu_custom_call" | custom-call | tf_op jit(solution)/shard_map/gather_branch/pallas_call | solution.py:140
  81.9 5.9 fusion.3
  98.3 8.1 %multiply_convert_fusion.1 = (bf16[2048,256]{1,0:T(8,128)(2,1)}, f32[2048,256]{1,0:T(8,128)}, f32[2048,256]{1,0:T(8,128)}) fusion(f32[256]{0:T(256)S(1)} %add.398, bf16[2048,1024]{1,0:T(8,128)(2,1)S(1)} %bitcast.255, bf16[2,1024,448]{1,2,0:T(8,128)(2,1)} %all-gather.6.cloned.1.call-done), kind=kOutput, calls=%fused_computation.50 | convolution fusion | flops 1108344832 | bytes 9962496 | tf_op jit(solution)/shard_map/dot_general | solution.py:646
  114.3 20.0 %attend.2 = (f32[2048,128]{1,0:T(8,128)S(1)}, f32[2048,128]{1,0:T(8,128)S(1)}) custom-call(s32[64]{0:T(128)S(1)} %pad_add_fusion.1.source_ref, s32[32]{0:T(128)S(1)} %get-tuple-element.101.order_ref, s32[32]{0:T(128)S(1)} %get-tuple-element.100.number_ref, bf16[2048,128]{1,0:T(8,128)(2,1)S(1)} %concatenate.119.q_ref, ...), custom_call_target="tpu_custom_call" | custom-call | tf_op jit(solution)/shard_map/attend/pallas_call | solution.py:374
  138.3 25.7 %scatter_out.2 = f32[128,1024]{1,0:T(8,128)S(1)} custom-call(bf16[16,128,1024]{2,1,0:T(8,128)(2,1)S(1)} %bitcast.234), custom_call_target="tpu_custom_call" | custom-call | tf_op jit(solution)/shard_map/scatter_out/pallas_call | solution.py:275
  165.8 24.1 %gather_normed.3 = bf16[16,128,1024]{2,1,0:T(8,128)(2,1)} custom-call(bf16[128,1024]{1,0:T(8,128)(2,1)} %fusion.62.own_ref), custom_call_target="tpu_custom_call" | custom-call | tf_op jit(solution)/shard_map/gather_normed/pallas_call | solution.py:140
  200.4 5.5 multiply_convert_fusion
  212.3 20.2 %attend.3 = (f32[2048,128]{1,0:T(8,128)S(1)}, f32[2048,128]{1,0:T(8,128)S(1)}) custom-call(s32[64]{0:T(128)S(1)} %pad_add_fusion.1.source_ref, s32[32]{0:T(128)S(1)} %get-tuple-element.101.order_ref, s32[32]{0:T(128)S(1)} %get-tuple-element.100.number_ref, bf16[2048,128]{1,0:T(8,128)(2,1)S(1)} %concatenate.126.q_ref, ...), custom_call_target="tpu_custom_call" | custom-call | tf_op jit(solution)/shard_map/attend/pallas_call | solution.py:374
  236.8 23.1 %attend_back.2 = (f32[2048,128]{1,0:T(8,128)S(1)}, bf16[4096,128]{1,0:T(8,128)(2,1)S(1)}) custom-call(s32[64]{0:T(128)S(1)} %pad_add_fusion.1.source_ref, s32[32]{0:T(128)S(1)} %get-tuple-element.101.order_ref, s32[32]{0:T(128)S(1)} %get-tuple-element.100.number_ref, bf16[2048,128]{1,0:T(8,128)(2,1)S(1)} %concatenate.126.q_ref, ...), custom_call_target="tpu_custom_call" | custom-call | tf_op jit(solution)/shard_map/attend_back/pallas_call | solution.py:465
  263.7 22.1 %scatter_out.3 = f32[128,1024]{1,0:T(8,128)S(1)} custom-call(bf16[16,128,1024]{2,1,0:T(8,128)(2,1)S(1)} %bitcast.233), custom_call_target="tpu_custom_call" | custom-call | tf_op jit(solution)/shard_map/scatter_out/pallas_call | solution.py:275
  293.8 24.5 %scatter_normed.2 = f32[128,1024]{1,0:T(8,128)S(1)} custom-call(bf16[16,128,1024]{2,1,0:T(8,128)(2,1)S(1)} %bitcast.235), custom_call_target="tpu_custom_call" | custom-call | tf_op jit(solution)/shard_map/scatter_normed/pallas_call | solution.py:275
  320.4 22.3 %gather_branch.3 = bf16[16,128,1024]{2,1,0:T(8,128)(2,1)} custom-call(bf16[128,1024]{1,0:T(8,128)(2,1)} %get-tuple-element.103.own_ref), custom_call_target="tpu_custom_call" | custom-call | tf_op jit(solution)/shard_map/gather_branch/pallas_call | solution.py:140
  351.8 23.1 %attend_back.3 = (f32[2048,128]{1,0:T(8,128)S(1)}, bf16[4096,128]{1,0:T(8,128)(2,1)S(1)}) custom-call(s32[64]{0:T(128)S(1)} %pad_add_fusion.1.source_ref, s32[32]{0:T(128)S(1)} %get-tuple-element.101.order_ref, s32[32]{0:T(128)S(1)} %get-tuple-element.100.number_ref, bf16[2048,128]{1,0:T(8,128)(2,1)S(1)} %concatenate.119.q_ref, ...), custom_call_target="tpu_custom_call" | custom-call | tf_op jit(solution)/shard_map/attend_back/pallas_call | solution.py:465
  413.9 20.9 %scatter_normed.3 = f32[128,1024]{1,0:T(8,128)S(1)} custom-call(bf16[16,128,1024]{2,1,0:T(8,128)(2,1)S(1)} %bitcast.232), custom_call_target="tpu_custom_call" | custom-call | tf_op jit(solution)/shard_map/scatter_normed/pallas_call | solution.py:275
  440.1 124.6 %all-reduce.7.cloned.1.call-done = f32[2,12288]{1,0:T(2,128)} async-done(((f32[2,12288]{1,0:T(2,128)}), f32[2,12288]{1,0:T(2,128)}) %all-reduce.7.cloned.1.call-update) | async-done | bytes 98320 | tf_op jit(solution)/shard_map/psum | solution.py:762
  570.2 47.5 %gather_tall.1 = bf16[16,256,1024]{2,1,0:T(8,128)(2,1)} custom-call(bf16[256,1024]{1,0:T(8,128)(2,1)} %bitcast.263), custom_call_target="tpu_custom_call" | custom-call | tf_op jit(solution)/shard_map/gather_tall/pallas_call | solution.py:140
  617.7 6.7 slice.442
  624.4 11.4 %convert.109 = f32[16,2,2,64,1024]{4,3,2,1,0:T(8,128)} convert(bf16[16,2,2,64,1024]{4,3,2,1,0:T(8,128)(2,1)} %bitcast.237) | non-fusion elementwise | flops 4194304 | bytes 25165824 | tf_op jit(solution)/shard_map/convert_element_type | solution.py:753
  653.3 49.2 %gather_wide.1 = bf16[16,512,448]{2,1,0:T(8,128)(2,1)} custom-call(bf16[512,448]{1,0:T(8,128)(2,1)} %bitcast.264), custom_call_target="tpu_custom_call" | custom-call | tf_op jit(solution)/shard_map/gather_wide/pallas_call | solution.py:140
  702.5 11.9 %copy.206 = bf16[16,512,448]{1,2,0:T(8,128)(2,1)} copy(bf16[16,512,448]{2,1,0:T(8,128)(2,1)} %gather_wide.1) | data formatting | bytes 14680064 | tf_op jit(solution)/shard_map/gather_wide/pallas_call | solution.py:140
  714.4 11.1 %reshape.333 = bf16[16,2,256,7,64]{2,1,4,3,0:T(2,128)(2,1)} reshape(bf16[16,512,448]{1,2,0:T(8,128)(2,1)} %copy.206) | data formatting | bytes 14680064 | tf_op jit(solution)/shard_map/reshape | solution.py:748
  737.4 6.6 copy.213
  744.0 8.9 %copy.214 = f32[2,256,4096]{2,1,0:T(8,128)} copy(f32[2,256,4096]{1,2,0:T(8,128)} %slice_convert_fusion) | data formatting | bytes 16777216
  (399 shorter events, 163.7 us)
Async XLA Ops:
  7.2 80.6 %all-gather.6.cloned.1.call-start = ((), (), s32[]{:S(2)}) async-start(), calls=%async_computation.2 | async-start | bytes 2293760 | tf_op jit(solution)/shard_map/all_gather | solution.py:568
  11.6 94.9 %all-gather.8.cloned.1.call-start = ((), (), s32[]{:S(2)}) async-start(), calls=%async_computation.7 | async-start | bytes 2621440 | tf_op jit(solution)/shard_map/all_gather | solution.py:569
  13.6 422.6 %reduce-scatter.5.cloned.1.call-start = ((), (), s32[]{:S(2)}) async-start(), calls=%async_computation.5 | async-start | bytes 1310720 | tf_op jit(solution)/shard_map/reduce_scatter | solution.py:737
  20.8 33.9 %copy-start.69 = (f32[128]{0:T(128)}, f32[128]{0:T(128)S(1)}, u32[]{:S(2)}) copy-start(f32[128]{0:T(128)S(1)} %broadcast_multiply_fusion.6) | copy-start | bytes 1540
  21.1 33.7 %copy-start.75 = (f32[128]{0:T(128)}, f32[128]{0:T(128)S(1)}, u32[]{:S(2)}) copy-start(f32[128]{0:T(128)S(1)} %add_rsqrt_fusion.1) | copy-start | bytes 1540
  22.3 167.6 %copy-start.51 = (f32[1,4,256]{2,0,1:T(1,128)}, f32[1,4,256]{2,0,1:T(1,128)S(1)}, u32[]{:S(2)}) copy-start(f32[1,4,256]{2,0,1:T(1,128)S(1)} %get-tuple-element.176) | copy-start | bytes 12292
  22.4 167.6 %copy-start.54 = (f32[1,4,256]{2,0,1:T(1,128)}, f32[1,4,256]{2,0,1:T(1,128)S(1)}, u32[]{:S(2)}) copy-start(f32[1,4,256]{2,0,1:T(1,128)S(1)} %get-tuple-element.175) | copy-start | bytes 12292
  22.4 167.5 %copy-start.58 = (f32[1,4,256]{2,0,1:T(1,128)}, f32[1,4,256]{2,0,1:T(1,128)S(1)}, u32[]{:S(2)}) copy-start(f32[1,4,256]{2,0,1:T(1,128)S(1)} %get-tuple-element.178) | copy-start | bytes 12292
  22.4 167.5 %copy-start.62 = (f32[1,4,256]{2,0,1:T(1,128)}, f32[1,4,256]{2,0,1:T(1,128)S(1)}, u32[]{:S(2)}) copy-start(f32[1,4,256]{2,0,1:T(1,128)S(1)} %get-tuple-element.177) | copy-start | bytes 12292
  22.6 59.2 %copy-start.49 = (f32[1,4,256]{2,0,1:T(1,128)}, f32[1,4,256]{2,0,1:T(1,128)S(1)}, u32[]{:S(2)}) copy-start(f32[1,4,256]{2,0,1:T(1,128)S(1)} %get-tuple-element.180) | copy-start | bytes 12292
  22.7 59.2 %copy-start.60 = (f32[1,4,256]{2,0,1:T(1,128)}, f32[1,4,256]{2,0,1:T(1,128)S(1)}, u32[]{:S(2)}) copy-start(f32[1,4,256]{2,0,1:T(1,128)S(1)} %get-tuple-element.182) | copy-start | bytes 12292
  22.7 59.2 %copy-start.64 = (f32[1,4,256]{2,0,1:T(1,128)}, f32[1,4,256]{2,0,1:T(1,128)S(1)}, u32[]{:S(2)}) copy-start(f32[1,4,256]{2,0,1:T(1,128)S(1)} %get-tuple-element.181) | copy-start | bytes 12292
  24.5 68.2 %copy-start.6 = (f32[2048,16]{1,0:T(8,128)}, f32[2048,16]{1,0:T(8,128)S(1)}, u32[]{:S(2)}) copy-start(f32[2048,16]{1,0:T(8,128)S(1)} %copy.188) | copy-start | bytes 393220
  24.8 67.9 %copy-start.10 = (f32[2048,16]{1,0:T(8,128)}, f32[2048,16]{1,0:T(8,128)S(1)}, u32[]{:S(2)}) copy-start(f32[2048,16]{1,0:T(8,128)S(1)} %copy.189) | copy-start | bytes 393220
  94.8 18.0 %collective-permute-start = (bf16[2048,128]{1,0:T(8,128)(2,1)}, bf16[2048,128]{1,0:T(8,128)(2,1)}, u32[]{:S(2)}, u32[]{:S(2)}) collective-permute-start(bf16[2048,128]{1,0:T(8,128)(2,1)} %pad_maximum_fusion.6), channel_id=1, source_target_pairs={{0,4},{4,0},{8,12},{12,8},{16,20},{20,16},{24,28},{28,24},{32,36},... | collective-permute-start | bytes 1572872 | tf_op jit(solution)/shard_map/ppermute | solution.py:530
  198.9 13.1 %collective-permute-start.1 = (bf16[2048,128]{1,0:T(8,128)(2,1)S(1)}, bf16[2048,128]{1,0:T(8,128)(2,1)S(1)}, u32[]{:S(2)}, u32[]{:S(2)}) collective-permute-start(bf16[2048,128]{1,0:T(8,128)(2,1)S(1)} %pad_maximum_fusion.8), channel_id=1, source_target_pairs={{0,4},{4,0},{8,12},{12,8},{16,20},{20,16},{24,28},{28,24},{32,36},... | collective-permute-start | bytes 1572872 | tf_op jit(solution)/shard_map/ppermute | solution.py:530
  260.2 25.8 %collective-permute-start.2 = (bf16[2048,128]{1,0:T(8,128)(2,1)S(1)}, bf16[2048,128]{1,0:T(8,128)(2,1)S(1)}, u32[]{:S(2)}, u32[]{:S(2)}) collective-permute-start(bf16[2048,128]{1,0:T(8,128)(2,1)S(1)} %slice.359), channel_id=1, source_target_pairs={{0,4},{4,0},{8,12},{12,8},{16,20},{20,16},{24,28},{28,24},{32,36},... | collective-permute-start | bytes 1572872 | tf_op jit(solution)/shard_map/ppermute | solution.py:530
  349.9 87.2 %all-reduce.9.cloned.1.call-start = ((), (), s32[]{:S(2)}) async-start(), calls=%async_computation.6 | async-start | bytes 524288 | tf_op jit(solution)/shard_map/psum | solution.py:740
  376.0 17.1 %collective-permute-start.3 = (bf16[2048,128]{1,0:T(8,128)(2,1)}, bf16[2048,128]{1,0:T(8,128)(2,1)}, u32[]{:S(2)}, u32[]{:S(2)}) collective-permute-start(bf16[2048,128]{1,0:T(8,128)(2,1)} %slice.370), channel_id=1, source_target_pairs={{0,4},{4,0},{8,12},{12,8},{16,20},{20,16},{24,28},{28,24},{32,36},... | collective-permute-start | bytes 1572872 | tf_op jit(solution)/shard_map/ppermute | solution.py:530
  384.8 179.9 %all-reduce.7.cloned.1.call-start = ((), (), s32[]{:S(2)}) async-start(), calls=%async_computation.3 | async-start | bytes 196608 | tf_op jit(solution)/shard_map/psum | solution.py:762
  406.1 232.8 %reduce-scatter.3.cloned.1.call-start = ((), (), s32[]{:S(2)}) async-start(), calls=%async_computation.4 | async-start | bytes 2293760 | tf_op jit(solution)/shard_map/reduce_scatter | solution.py:734
  438.1 131.1 %collective-permute-start.5 = (bf16[2,128,1024]{2,1,0:T(8,128)(2,1)S(1)}, bf16[2,128,1024]{2,1,0:T(8,128)(2,1)S(1)}, u32[]{:S(2)}, u32[]{:S(2)}) collective-permute-start(bf16[2,128,1024]{2,1,0:T(8,128)(2,1)S(1)} %constant_dynamic-update-slice_fusion.13), channel_id=1, source_target_pairs={{0,4},{4,0},{8,12},{12,8},{16,20},{20,16},{24,28},{28,24},{32,36},... | collective-permute-start | bytes 1572872 | tf_op jit(solution)/shard_map/ppermute | solution.py:530
  565.4 187.5 %copy-start.68 = (f32[2,256]{1,0:T(2,128)}, f32[2,256]{1,0:T(2,128)S(1)}, u32[]{:S(2)}) copy-start(f32[2,256]{1,0:T(2,128)S(1)} %get-tuple-element.222) | copy-start | bytes 6148
  638.9 13.2 %collective-permute-start.4 = (bf16[2,256,448]{1,2,0:T(8,128)(2,1)}, bf16[2,256,448]{1,2,0:T(8,128)(2,1)S(1)}, u32[]{:S(2)}, u32[]{:S(2)}) collective-permute-start(bf16[2,256,448]{1,2,0:T(8,128)(2,1)} %reduce-scatter.3.cloned.1.call-done), channel_id=1, source_target_pairs={{0,4},{4,0},{8,12},{12,8},{16,20},{20,16},{24,28},{28,24},{32,36},... | collective-permute-start | bytes 1376264 | tf_op jit(solution)/shard_map/ppermute | solution.py:530
  (75 other events, 451.3 us)
Sparse Core Ops, SparseCore 0:
  11.7 27.2 all-gather.5
  40.6 30.3 all-gather.7
  350.0 20.3 reduce-scatter.4
  384.9 34.5 all-reduce.8
  424.0 140.6 all-reduce.6
  567.7 21.8 reduce-scatter.2

commit v2 on v1

v2 whole, which is shorter than its diff:
```python
import functools

import jax
import jax.numpy as jnp
from jax import lax
from jax.experimental import pallas as pl
from jax.experimental.pallas import tpu as pltpu
from jax.sharding import PartitionSpec as P

HEADS = 16
HEAD = 64
ROT = 16
BLK = 64
SIDE = 4
EPS = 1e-05
NEGATIVE = -1e30
MESH = pl.DeviceIdType.MESH
F32 = jnp.float32
BF16 = jnp.bfloat16
TILE = 256
KEYS = 512
PART = 64
PARTS = 13
LANES = 256
OUT_PART = 11


def place():
    slot = lax.axis_index("ctx")
    return slot // 8, (slot // 2) % SIDE, slot % 2


def device(x, y, z):
    return {"ctx": ((x % SIDE) * SIDE + (y % SIDE)) * 2 + z}


class Grid:
    def __init__(self):
        self.x, self.y, self.z = place()

    def spot(self, half, dp, dq):
        dx, dy = (dp, dq) if half == 0 else (dq, dp)
        return (self.x + dx + SIDE) % SIDE, (self.y + dy + SIDE) % SIDE

    def rank(self, half, dp, dq):
        x, y = self.spot(half, dp, dq)
        return x * SIDE + y

    def device(self, half, dp, dq):
        x, y = self.spot(half, dp, dq)
        return device(x, y, self.z)

    def barrier(self, others=()):
        gate = pltpu.get_barrier_semaphore()
        partners = [self.device(0, *step) for step in ((1, 0), (-1, 0), (0, 1), (0, -1))]
        partners += others
        for partner in partners:
            pl.semaphore_signal(gate, inc=1, device_id=partner, device_id_type=MESH)
        pl.semaphore_wait(gate, len(partners))


def gather_half(grid, half, own_ref, all_ref, send_sem, recv_sem):
    rows = own_ref.shape[0]
    half_rows, quarter = rows // 2, rows // 4
    sends = []

    def view(dp, dq, low, count):
        return all_ref.at[grid.rank(half, dp, dq), pl.ds(half * half_rows + low, count)]

    def start(event, to, block, low, count, own=False):
        source = (
            own_ref.at[pl.ds(half * half_rows + low, count)]
            if own
            else view(*block, low, count)
        )
        copy = pltpu.make_async_remote_copy(
            src_ref=source,
            dst_ref=view(*block, low, count),
            send_sem=send_sem.at[half, event],
            recv_sem=recv_sem.at[half, event],
            device_id=grid.device(half, *to),
            device_id_type=MESH,
        )
        copy.start()
        sends.append(copy)

    def arrive(event, block, low, count):
        there = view(*block, low, count)
        pltpu.make_async_remote_copy(
            src_ref=there,
            dst_ref=there,
            send_sem=send_sem.at[half, event],
            recv_sem=recv_sem.at[half, event],
            device_id=grid.device(half, 1, 0),
            device_id_type=MESH,
        ).wait_recv()

    def spread(column, dp, own=False):
        start(4 + 4 * column, (0, 1), (dp, 0), 0, half_rows, own)
        start(5 + 4 * column, (0, -1), (dp, 0), 0, half_rows, own)

    start(0, (1, 0), (0, 0), 0, half_rows, True)
    start(1, (-1, 0), (0, 0), 0, half_rows, True)
    spread(0, 0, True)
    yield
    arrive(0, (-1, 0), 0, half_rows)
    start(2, (1, 0), (-1, 0), 0, quarter)
    spread(1, -1)
    arrive(1, (1, 0), 0, half_rows)
    start(3, (-1, 0), (1, 0), quarter, quarter)
    spread(2, 1)
    yield
    arrive(2, (2, 0), 0, quarter)
    arrive(3, (2, 0), quarter, quarter)
    spread(3, 2)
    yield
    steps = (0, -1, 1, 2)
    for column in range(4):
        arrive(4 + 4 * column, (steps[column], -1), 0, half_rows)
        start(6 + 4 * column, (0, 1), (steps[column], -1), 0, quarter)
        arrive(5 + 4 * column, (steps[column], 1), 0, half_rows)
        start(7 + 4 * column, (0, -1), (steps[column], 1), quarter, quarter)
        yield
    for column in range(4):
        arrive(6 + 4 * column, (steps[column], 2), 0, quarter)
        arrive(7 + 4 * column, (steps[column], 2), quarter, quarter)
        if column % 2 == 0:
            yield
    for copy in sends:
        copy.wait_send()


GATHER_STEPS = 10


def gather_steps(grid, own_ref, all_ref, send_sem, recv_sem):
    halves = [
        gather_half(grid, half, own_ref, all_ref, send_sem, recv_sem) for half in (0, 1)
    ]
    for step in range(GATHER_STEPS):
        for half in halves:
            next(half, None)
        if step < GATHER_STEPS - 1:
            yield


def run(steps, count=None):
    while count is None or count > 0:
        if next(steps, StopIteration) is StopIteration:
            return
        count = None if count is None else count - 1


def scatter_steps(grid, part_ref, out_ref, land_half, land_full, stage, total, send_sem, recv_sem):
    rows = part_ref.shape[1]
    half_rows, quarter = rows // 2, rows // 4
    sends = []
    steps = (2, -1, 1, 0)

    def start(half, event, source, target, to):
        copy = pltpu.make_async_remote_copy(
            src_ref=source,
            dst_ref=target,
            send_sem=send_sem.at[half, event],
            recv_sem=recv_sem.at[half, event],
            device_id=grid.device(half, *to),
            device_id_type=MESH,
        )
        copy.start()
        sends.append(copy)

    def arrive(half, event, target):
        pltpu.make_async_remote_copy(
            src_ref=target,
            dst_ref=target,
            send_sem=send_sem.at[half, event],
            recv_sem=recv_sem.at[half, event],
            device_id=grid.device(half, 1, 0),
            device_id_type=MESH,
        ).wait_recv()

    def first(half, column):
        def piece(dq, low, count):
            return part_ref.at[
                grid.rank(half, steps[column], dq), pl.ds(half * half_rows + low, count)
            ]

        return piece

    def second(half):
        return lambda dp, low, count: total.at[half, steps.index(dp), pl.ds(low, count)]

    def along(step):
        return (0, step)

    def across(step):
        return (step, 0)

    def opposite(half, column, piece, step):
        for side, low in ((0, 0), (1, quarter)):
            start(
                half,
                4 * column + side,
                piece(2, low, quarter),
                land_half.at[half, column, side],
                step(1 - 2 * side),
            )

    def neighbours(half, column, piece, step):
        for side in (0, 1):
            land = land_half.at[half, column, side]
            arrive(half, 4 * column + side, land)
            low, other = side * quarter, (1 - side) * quarter
            toward = 1 - 2 * side
            stage[half, column, side, low : low + quarter] = (
                piece(toward, low, quarter)[...].astype(F32) + land[...].astype(F32)
            ).astype(BF16)
            stage[half, column, side, other : other + quarter] = piece(toward, other, quarter)[...]
            start(
                half,
                4 * column + 2 + side,
                stage.at[half, column, side],
                land_full.at[half, column, side],
                step(toward),
            )

    def settle(half, column, own):
        for side in (0, 1):
            arrive(half, 4 * column + 2 + side, land_full.at[half, column, side])
        return (
            own[...].astype(F32)
            + land_full[half, column, 0].astype(F32)
            + land_full[half, column, 1].astype(F32)
        )

    for column in range(4):
        for half in (0, 1):
            opposite(half, column, first(half, column), along)
    yield
    for column in range(4):
        for half in (0, 1):
            neighbours(half, column, first(half, column), along)
        if column % 2:
            yield
    for column in range(4):
        for half in (0, 1):
            total[half, column] = settle(
                half, column, first(half, column)(0, 0, half_rows)
            ).astype(BF16)
            if column == 0:
                opposite(half, 4, second(half), across)
            if column == 2:
                neighbours(half, 4, second(half), across)
        yield
    for half in (0, 1):
        out_ref[pl.ds(half * half_rows, half_rows)] = settle(half, 4, total.at[half, 3])
    for copy in sends:
        copy.wait_send()


SCATTER_STEPS = 8


def scatter_scratch(rows, width):
    half_rows, quarter = rows // 2, rows // 4
    return [
        pltpu.VMEM((2, 5, 2, quarter, width), BF16),
        pltpu.VMEM((2, 5, 2, half_rows, width), BF16),
        pltpu.VMEM((2, 5, 2, half_rows, width), BF16),
        pltpu.VMEM((2, 4, half_rows, width), BF16),
        pltpu.SemaphoreType.DMA((2, 20)),
        pltpu.SemaphoreType.DMA((2, 20)),
    ]


def skip_two(index):
    return index + index // 2


def far_spot(index):
    inside = index < 4
    return jnp.where(inside, index, 2), jnp.where(inside, 2, skip_two(jnp.maximum(index - 4, 0)))


def near_spot(index):
    return skip_two(index // 3), skip_two(index % 3)


def over_places(grid, spot, count, body):
    def one(index, unused):
        dx, dy = spot(index)
        body(((grid.x + dx) % SIDE) * SIDE + (grid.y + dy) % SIDE)
        return unused

    lax.fori_loop(0, count, one, 0)


def follow(grid, gather, block, ready=None):
    def places(*steps):
        def spot(index):
            dx, dy = jnp.int32(steps[0][0]), jnp.int32(steps[0][1])
            for i in range(1, len(steps)):
                dx = jnp.where(index == i, steps[i][0], dx)
                dy = jnp.where(index == i, steps[i][1], dy)
            return dx, dy

        over_places(grid, spot, len(steps), block)

    run(gather, 2)
    if ready is not None:
        ready()
    places((0, 0))
    next(gather)
    places((0, 1), (0, 3), (1, 0), (3, 0))
    next(gather)
    next(gather)
    places((1, 1), (1, 3), (3, 1), (3, 3))
    next(gather)
    next(gather)
    places((0, 2), (2, 0))
    next(gather)
    places((1, 2), (3, 2), (2, 1), (2, 3))
    run(gather)
    places((2, 2))


SQRT_HALF = 0.7071067811865476
DENSITY = 0.3989422804014327


def standardize(stream):
    row_mean = jnp.mean(stream, -1, keepdims=True)
    centered = stream - row_mean
    spread = jnp.mean(centered * centered, -1, keepdims=True)
    inverse = lax.rsqrt(spread + EPS)
    return (centered * inverse, inverse)


def dots(a, b, da, db):
    return lax.dot_general(a, b, (((da,), (db,)), ((), ())), preferred_element_type=F32)


def rotate(values, cosines, sines):
    lane = lax.broadcasted_iota(jnp.int32, values.shape, 1)
    half_dims = ROT // 2
    up = pltpu.roll(values, 2 * HEAD - half_dims, 1)
    down = pltpu.roll(values, half_dims, 1)
    return values * cosines + jnp.where(lane < half_dims, -up, down) * sines


def block_rows(rank, rows):
    return pl.ds(pl.multiple_of(rank * rows, rows), rows)


def share_partners():
    shard = lax.axis_index("fsdp")
    return [{"fsdp": shard + 1 - 2 * (shard % 2)}, {"fsdp": (shard + 2) % 4}]


def share_steps(items, send_sem, recv_sem):
    shard = lax.axis_index("fsdp")
    sibling = shard + 1 - 2 * (shard % 2)
    mate = (shard + 2) % 4
    third = (sibling + 2) % 4
    sends = []

    def copy(item, source, target, event, to):
        return pltpu.make_async_remote_copy(
            src_ref=source,
            dst_ref=target,
            send_sem=send_sem.at[item, event],
            recv_sem=recv_sem.at[item, event],
            device_id={"fsdp": to},
            device_id_type=MESH,
        )

    def start(*args):
        made = copy(*args)
        made.start()
        sends.append(made)

    for item, (own, every) in enumerate(items):
        start(item, own, every.at[shard], 0, mate)
        start(item, own, every.at[shard], 1, sibling)
        every[shard] = own[...]
    yield
    for item, (own, every) in enumerate(items):
        copy(item, own, every.at[mate], 0, mate).wait_recv()
        start(item, every.at[mate], every.at[mate], 2, sibling)
        yield
    for item, (own, every) in enumerate(items):
        copy(item, own, every.at[sibling], 1, sibling).wait_recv()
        copy(item, own, every.at[third], 2, sibling).wait_recv()
        yield
    for made in sends:
        made.wait_send()


def share_sems(items):
    return [pltpu.SemaphoreType.DMA((items, 3)), pltpu.SemaphoreType.DMA((items, 3))]


def stack_tall(tall_all, tall_ref):
    for part in range(4):
        tall_ref[part * HEAD : (part + 1) * HEAD] = tall_all[part, :HEAD]
    tall_ref[4 * HEAD : 5 * HEAD] = jnp.zeros((HEAD, tall_ref.shape[1]), BF16)
    tall_ref[5 * HEAD :] = tall_all[place()[0], HEAD:]


def enter_kernel(shares, *refs):
    (stream_ref, scale_ref, bias_ref, cos_ref, sin_ref, given_ref), refs = refs[:6], refs[6:]
    (normed_ref, q_ref, kv_ref, active_ref, slope_ref), refs = refs[:5], refs[5:]
    if shares:
        (wide_ref, own, send_sem, recv_sem), share_refs = refs[:4], refs[4:]
    else:
        own, send_sem, recv_sem = refs
        wide_ref = given_ref
    grid = Grid()
    rows, width = stream_ref.shape
    own[...] = standardize(stream_ref[...])[0].astype(BF16)
    normed_ref[grid.rank(0, 0, 0)] = own[...]
    grid.barrier(share_partners() if shares else ())
    sharing = None
    if shares:
        sharing = share_steps([(given_ref, wide_ref)], *share_refs)
        next(sharing)
    gather = gather_steps(grid, own, normed_ref, send_sem, recv_sem)
    next(gather)

    def block(rank):
        place_rows = block_rows(rank, rows)
        plain = normed_ref[rank].astype(F32)
        first = (plain * scale_ref[0:1] + scale_ref[2:3]).astype(BF16)
        second = (plain * scale_ref[1:2] + scale_ref[3:4]).astype(BF16)
        weight = wide_ref[...].reshape(width, 8 * HEAD)
        mixed = dots(first, weight[:, : 4 * HEAD], 1, 0) + bias_ref[:, : 4 * HEAD]
        hidden = dots(second, weight[:, 4 * HEAD :], 1, 0) + bias_ref[:, 4 * HEAD :]
        cosines, sines = cos_ref[place_rows, :], sin_ref[place_rows, :]
        kv_ref[place_rows, :] = rotate(mixed[:, : 2 * HEAD], cosines, sines).astype(BF16)
        q_ref[place_rows, :] = (rotate(mixed[:, 2 * HEAD :], cosines, sines) * 0.125).astype(BF16)
        share = 0.5 * (1.0 + lax.erf(hidden * SQRT_HALF))
        active_ref[place_rows, :] = (hidden * share).astype(BF16)
        slope_ref[place_rows, :] = share + hidden * (DENSITY * jnp.exp(-0.5 * hidden * hidden))

    def ready():
        if shares:
            run(sharing)

    follow(grid, gather, block, ready)


def enter(stream, scale, bias, cosines, sines, wide, shares, number):
    rows, width = stream.shape
    total = 16 * rows
    shapes = [
        jax.ShapeDtypeStruct((16, rows, width), BF16),
        jax.ShapeDtypeStruct((total, 2 * HEAD), BF16),
        jax.ShapeDtypeStruct((total, 2 * HEAD), BF16),
        jax.ShapeDtypeStruct((total, 4 * HEAD), BF16),
        jax.ShapeDtypeStruct((total, 4 * HEAD), F32),
    ]
    scratch = [
        pltpu.VMEM((rows, width), BF16),
        pltpu.SemaphoreType.DMA((2, 20)),
        pltpu.SemaphoreType.DMA((2, 20)),
    ]
    if shares:
        shapes.append(jax.ShapeDtypeStruct((4,) + wide.shape, BF16))
        scratch += share_sems(1)
    return pl.pallas_call(
        functools.partial(enter_kernel, shares),
        out_shape=shapes,
        in_specs=[pl.BlockSpec(memory_space=pltpu.VMEM)] * 6,
        out_specs=[pl.BlockSpec(memory_space=pltpu.VMEM)] * len(shapes),
        scratch_shapes=scratch,
        name="enter",
        compiler_params=pltpu.CompilerParams(
            collective_id=number, has_side_effects=True, vmem_limit_bytes=48 << 20
        ),
    )(stream, scale, bias, cosines, sines, wide)


def leave_steps(
    grid, active_ref, context_ref, tall_ref, stream_ref, bias_ref, out_ref, parts, total_rows, scratch
):
    rows = stream_ref.shape[0]

    def block(rank):
        place_rows = block_rows(rank, rows)
        both = jnp.concatenate(
            [active_ref[place_rows, :], context_ref[place_rows, :].astype(BF16)], 1
        )
        parts[rank] = dots(both, tall_ref[...], 1, 0).astype(BF16)

    scatter = scatter_steps(grid, parts, total_rows, *scratch)
    over_places(grid, far_spot, 7, block)
    next(scatter)
    over_places(grid, near_spot, 9, block)
    yield
    yield from scatter
    out_ref[...] = (stream_ref[...] + total_rows[...] + bias_ref[...]).astype(out_ref.dtype)


def leave_kernel(*refs):
    given, (wide_own, tall_own), made = refs[:5], refs[5:7], refs[7:10]
    out_ref, wide_ref, tall_ref = made
    (parts, total_rows, tall_all), refs = refs[10:13], refs[13:]
    grid = Grid()
    grid.barrier(share_partners())
    sharing = share_steps([(wide_own, wide_ref), (tall_own, tall_all)], *refs[:2])
    next(sharing)
    steps = leave_steps(grid, *given, out_ref, parts, total_rows, refs[2:])
    run(steps, 4)
    run(sharing, 1)
    run(steps, 2)
    run(sharing, 1)
    run(steps)
    run(sharing)
    stack_tall(tall_all, tall_ref)


def leave(active, context, tall, stream, bias, wide_own, tall_own, number):
    rows, width = stream.shape
    vmem = pl.BlockSpec(memory_space=pltpu.VMEM)
    return pl.pallas_call(
        leave_kernel,
        out_shape=[
            jax.ShapeDtypeStruct((rows, width), F32),
            jax.ShapeDtypeStruct((4,) + wide_own.shape, BF16),
            jax.ShapeDtypeStruct((6 * HEAD, width), BF16),
        ],
        in_specs=[vmem] * 7,
        out_specs=[vmem] * 3,
        scratch_shapes=[
            pltpu.VMEM((16, rows, width), BF16),
            pltpu.VMEM((rows, width), F32),
            pltpu.VMEM((4,) + tall_own.shape, BF16),
        ]
        + share_sems(2)
        + scatter_scratch(rows, width),
        name="leave",
        compiler_params=pltpu.CompilerParams(
            collective_id=number, has_side_effects=True, vmem_limit_bytes=48 << 20
        ),
    )(active, context, tall, stream, bias, wide_own, tall_own)


def back_enter_kernel(gathers, folds, *refs):
    grad_ref, active_ref, context_ref, slope_ref, normed_ref, tall_ref = refs[:6]
    refs = refs[6:]
    if folds:
        (in_ref, quarter_ref), refs = refs[:2], refs[2:]
    pull_ref, offset_ref, hidden_ref, down_ref, out_ref, up_ref, up_bias_ref = refs[:7]
    refs = refs[7:]
    if folds:
        (folded_ref,), refs = refs[:1], refs[1:]
    tall_sum, refs = refs[0], refs[1:]
    grid = Grid()
    tall_sum[...] = jnp.zeros_like(tall_sum)
    up_ref[...] = jnp.zeros_like(up_ref)
    up_bias_ref[...] = jnp.zeros_like(up_bias_ref)
    rows = grad_ref.shape[-2]

    if gathers:
        own, all_rows, send_sem, recv_sem = refs[:4]
        refs = refs[4:]
        own[...] = grad_ref[...].astype(BF16)
        all_rows[grid.rank(0, 0, 0)] = own[...]
        if folds:
            fold_barrier(grid)
        else:
            grid.barrier()
        gather = gather_steps(grid, own, all_rows, send_sem, recv_sem)
        next(gather)
    else:
        all_rows = grad_ref

    def block(rank):
        place_rows = block_rows(rank, rows)
        branch = all_rows[rank]
        back = dots(branch, tall_ref[...], 1, 1)
        hidden_grad = (back[:, : 4 * HEAD] * slope_ref[place_rows, :]).astype(BF16)
        pull = back[:, 4 * HEAD :].astype(BF16)
        hidden_ref[place_rows, :] = hidden_grad
        pull_ref[place_rows, :] = pull
        context = context_ref[place_rows, :]
        offset = jnp.sum(pull.astype(F32) * context, 1, keepdims=True)
        offset_ref[place_rows, :] = jnp.broadcast_to(offset, (rows, 2 * HEAD))
        both = jnp.concatenate([active_ref[place_rows, :], context.astype(BF16)], 1)
        ones = jnp.ones((rows, 2 * HEAD), BF16)
        tall_sum[...] += dots(both, branch, 0, 0)
        up_ref[...] += dots(hidden_grad, normed_ref[rank], 0, 0)
        up_bias_ref[...] += dots(hidden_grad, ones, 0, 0)

    if gathers:
        if folds:
            fold = fold_steps(grid, in_ref, quarter_ref, folded_ref, refs)
            next(fold)

            def together():
                for step in range(1, GATHER_STEPS):
                    run(gather, 1)
                    if step in (1, 4, 6, 8, 9):
                        run(fold, 1)
                    yield
                run(gather)
                run(fold)

            follow(grid, together(), block)
        else:
            follow(grid, gather, block)
    else:

        def one(rank, unused):
            block(rank)
            return unused

        lax.fori_loop(0, 16, one, 0)
    for shard in range(4):
        for lanes in range(4):
            down_ref[shard, lanes * HEAD : (lanes + 1) * HEAD] = tall_sum[
                shard * HEAD : (shard + 1) * HEAD, lanes * LANES : (lanes + 1) * LANES
            ].astype(BF16)
            low = 5 * HEAD + shard * 16
            out_ref[shard, lanes * 16 : (lanes + 1) * 16] = tall_sum[
                low : low + 16, lanes * LANES : (lanes + 1) * LANES
            ].astype(BF16)


def back_enter(grad, active, context, slope, normed, tall, number=None, folding=None):
    rows, width = grad.shape[-2:]
    total = 16 * rows
    vmem = pl.BlockSpec(memory_space=pltpu.VMEM)
    given = [grad, active, context, slope, normed, tall]
    shapes = [
        jax.ShapeDtypeStruct((total, 2 * HEAD), BF16),
        jax.ShapeDtypeStruct((total, 2 * HEAD), F32),
        jax.ShapeDtypeStruct((total, 4 * HEAD), BF16),
        jax.ShapeDtypeStruct((4, 4 * HEAD, LANES), BF16),
        jax.ShapeDtypeStruct((4, HEAD, LANES), BF16),
        jax.ShapeDtypeStruct((4 * HEAD, width), F32),
        jax.ShapeDtypeStruct((4 * HEAD, 2 * HEAD), F32),
    ]
    scratch = [pltpu.VMEM((6 * HEAD, width), F32)]
    params = dict(vmem_limit_bytes=48 << 20)
    if number is not None:
        params.update(collective_id=number, has_side_effects=True)
        scratch += [
            pltpu.VMEM((rows, width), BF16),
            pltpu.VMEM((16, rows, width), BF16),
            pltpu.SemaphoreType.DMA((2, 20)),
            pltpu.SemaphoreType.DMA((2, 20)),
        ]
    if folding is not None:
        given += list(folding)
        shapes.append(jax.ShapeDtypeStruct(folding[0].shape[1:], BF16))
        scratch += fold_scratch(folding[0].shape[1])
    return pl.pallas_call(
        functools.partial(back_enter_kernel, number is not None, folding is not None),
        out_shape=shapes,
        in_specs=[vmem] * len(given),
        out_specs=[vmem] * len(shapes),
        scratch_shapes=scratch,
        name="back_enter",
        compiler_params=pltpu.CompilerParams(**params),
    )(*given)


def back_leave_kernel(
    query_grad_ref,
    pair_grad_ref,
    hidden_ref,
    normed_ref,
    wide_ref,
    scale_ref,
    cos_ref,
    sin_ref,
    stream_ref,
    grad_ref,
    up_ref,
    up_bias_ref,
    down_ref,
    new_ref,
    addend_ref,
    mixed,
    raw,
    raw_bias,
    parts,
    total_rows,
    *scratch,
):
    grid = Grid()
    rows, width = stream_ref.shape
    grid.barrier()
    lane = lax.broadcasted_iota(jnp.int32, (rows, 2 * HEAD), 1)
    ones = jnp.ones((rows, 2 * HEAD), BF16)

    def block(rank):
        place_rows = block_rows(rank, rows)
        cosines, sines = cos_ref[place_rows, :], -sin_ref[place_rows, :]
        pair = pair_grad_ref[place_rows, :]
        query = jnp.where(lane < HEAD, query_grad_ref[place_rows, :] * 0.125, 0.0)
        both = jnp.concatenate(
            [rotate(pair, cosines, sines), rotate(query, cosines, sines)], 1
        ).astype(BF16)
        mixed[place_rows, :] = both
        first = dots(both, wide_ref[:, : 4 * HEAD], 1, 1)
        second = dots(hidden_ref[place_rows, :], wide_ref[:, 4 * HEAD :], 1, 1)
        parts[rank] = (first * scale_ref[0:1] + second * scale_ref[1:2]).astype(BF16)

    scatter = scatter_steps(grid, parts, total_rows, *scratch)
    over_places(grid, far_spot, 7, block)
    next(scatter)
    over_places(grid, near_spot, 9, block)
    next(scatter)
    raw[...] = jnp.zeros_like(raw)
    raw_bias[...] = jnp.zeros_like(raw_bias)

    def sums(first, count):
        def one(rank, unused):
            place_rows = block_rows(rank, rows)
            both = mixed[place_rows, :]
            raw[...] += dots(both, normed_ref[rank], 0, 0)
            raw_bias[...] += dots(both, ones, 0, 0)
            return unused

        lax.fori_loop(first, first + count, one, 0)

    sums(0, 4)
    next(scatter)
    sums(4, 4)
    next(scatter)
    sums(8, 4)
    next(scatter)
    sums(12, 4)
    next(scatter)

    wide_t = jnp.transpose(wide_ref[:, : 4 * HEAD].astype(F32))
    up_t = jnp.transpose(wide_ref[:, 4 * HEAD :].astype(F32))
    mixed_bias, up_bias = raw_bias[:, 0:1], up_bias_ref[:, 0:1]
    first_raw, second_raw = raw[...], up_ref[...]
    vectors = [
        jnp.sum(wide_t * first_raw, 0, keepdims=True),
        jnp.sum(up_t * second_raw, 0, keepdims=True),
        jnp.sum(wide_t * mixed_bias, 0, keepdims=True),
        jnp.sum(up_t * up_bias, 0, keepdims=True),
        jnp.sum(grad_ref[...].astype(BF16).astype(F32), 0, keepdims=True),
    ]
    first_grad = (first_raw * scale_ref[0:1] + mixed_bias * scale_ref[2:3]).astype(BF16)
    second_grad = (second_raw * scale_ref[1:2] + up_bias * scale_ref[3:4]).astype(BF16)
    biases = [
        jnp.transpose(raw_bias[...])[0:1],
        jnp.transpose(up_bias_ref[...])[0:1],
    ]
    for shard in range(4):
        lanes = slice(shard * LANES, (shard + 1) * LANES)
        addend_ref[shard, : 3 * PART] = first_grad[: 3 * PART, lanes]
        addend_ref[shard, 3 * PART : 7 * PART] = second_grad[:, lanes]
        addend_ref[shard, 7 * PART : OUT_PART * PART] = down_ref[shard]
        tail = jnp.concatenate(
            [jnp.zeros((PART, LANES), F32)]
            + [vector[:, lanes] for vector in vectors]
            + biases
            + [jnp.zeros((PART - 7, LANES), F32)],
            0,
        )
        addend_ref[shard, OUT_PART * PART :] = tail.astype(BF16)
    next(scatter)
    run(scatter)
    normed, inverse = standardize(stream_ref[...])
    normed_grad = total_rows[...]
    new_ref[...] = grad_ref[...] + inverse * (
        normed_grad
        - jnp.mean(normed_grad, -1, keepdims=True)
        - normed * jnp.mean(normed_grad * normed, -1, keepdims=True)
    )


def back_leave(given, rows, width, number):
    vmem = pl.BlockSpec(memory_space=pltpu.VMEM)
    total = 16 * rows
    return pl.pallas_call(
        back_leave_kernel,
        out_shape=[
            jax.ShapeDtypeStruct((rows, width), F32),
            jax.ShapeDtypeStruct((4, PARTS * PART, LANES), BF16),
        ],
        in_specs=[vmem] * len(given),
        out_specs=[vmem] * 2,
        scratch_shapes=[
            pltpu.VMEM((total, 4 * HEAD), BF16),
            pltpu.VMEM((4 * HEAD, width), F32),
            pltpu.VMEM((4 * HEAD, 2 * HEAD), F32),
            pltpu.VMEM((16, rows, width), BF16),
            pltpu.VMEM((rows, width), F32),
        ]
        + scatter_scratch(rows, width),
        name="back_leave",
        compiler_params=pltpu.CompilerParams(
            collective_id=number, has_side_effects=True, vmem_limit_bytes=56 << 20
        ),
    )(*given)


def fold_partners(grid):
    shard = lax.axis_index("fsdp")
    return [
        {"fsdp": shard + 1 - 2 * (shard % 2)},
        {"fsdp": (shard + 2) % 4},
        {"ctx": lax.axis_index("ctx") + 1 - 2 * grid.z},
    ]


def fold_barrier(grid):
    shard = lax.axis_index("fsdp")
    at_home = grid.x == shard
    gate = pltpu.get_barrier_semaphore()
    partners = [grid.device(0, *step) for step in ((1, 0), (-1, 0), (0, 1), (0, -1))]
    partners += fold_partners(grid)
    for partner in partners:
        pl.semaphore_signal(gate, inc=1, device_id=partner, device_id_type=MESH)
    for other in range(4):

        @pl.when(jnp.logical_not(at_home & (shard == other)))
        def greet():
            pl.semaphore_signal(
                gate,
                inc=1,
                device_id={"ctx": (shard * SIDE + grid.y) * 2 + grid.z, "fsdp": other},
                device_id_type=MESH,
            )

    pl.semaphore_wait(gate, len(partners) + 4 - at_home.astype(jnp.int32))


def fold_steps(grid, in_ref, quarter_ref, own, scratch):
    land_core, sums, land_low, pair, land_high, land_out = scratch[:6]
    core_sem, low_sem, high_sem, out_send, out_recv = scratch[6:]
    x, y, z = grid.x, grid.y, grid.z
    shard = lax.axis_index("fsdp")
    low, core = shard // 2, shard % 2
    away = 1 - low
    sibling, mate, far = fold_partners(grid)
    at_home = x == shard
    half_rows = in_ref.shape[1] // 2

    def remote(source, target, send, recv, to):
        return pltpu.make_async_remote_copy(
            src_ref=source,
            dst_ref=target,
            send_sem=send,
            recv_sem=recv,
            device_id=to,
            device_id_type=MESH,
        )

    def added(a, b):
        return (a.astype(F32) + b.astype(F32)).astype(BF16)

    def out_copy(column):
        return remote(
            quarter_ref.at[column],
            land_out.at[shard],
            out_send.at[column],
            out_recv.at[shard],
            {"ctx": (column * SIDE + y) * 2 + z, "fsdp": x},
        )

    spans = [pl.ds(half * half_rows, half_rows) for half in (0, 1)]
    core_copies, low_copies, high_copies = {}, [], []
    for half, span in enumerate(spans):
        for part in (0, 1):
            core_copies[half, part] = remote(
                in_ref.at[part * 2 + 1 - core, span],
                land_core.at[part, span],
                core_sem.at[0, half, part],
                core_sem.at[1, half, part],
                sibling,
            )
            core_copies[half, part].start()
    for column in range(4):

        @pl.when(jnp.logical_not(at_home & (x == column)))
        def give():
            out_copy(column).start()

        @pl.when(at_home & (x == column))
        def keep():
            land_out[shard] = quarter_ref[column]

    yield
    for half, span in enumerate(spans):
        for part in (0, 1):
            core_copies[half, part].wait_recv()
        sums[1, span] = added(in_ref[away * 2 + core, span], land_core[away, span])
        copy = remote(
            sums.at[1, span], land_low.at[span], low_sem.at[0, half], low_sem.at[1, half], mate
        )
        copy.start()
        low_copies.append(copy)
        sums[0, span] = added(in_ref[low * 2 + core, span], land_core[low, span])
    yield
    for half, span in enumerate(spans):
        low_copies[half].wait_recv()
        pair[span] = added(sums[0, span], land_low[span])
        if half == 1:
            for other in range(4):

                @pl.when(jnp.logical_not(at_home & (shard == other)))
                def take():
                    remote(
                        land_out.at[other],
                        land_out.at[other],
                        out_send.at[other],
                        out_recv.at[other],
                        mate,
                    ).wait_recv()

            total = land_out[0].astype(F32)
            for other in range(1, 4):
                total = total + land_out[other].astype(F32)
            pair[OUT_PART * PART : (OUT_PART + 1) * PART] = total.astype(BF16)
        copy = remote(
            pair.at[span], land_high.at[span], high_sem.at[0, half], high_sem.at[1, half], far
        )
        copy.start()
        high_copies.append(copy)
        yield
    for half, span in enumerate(spans):
        high_copies[half].wait_recv()
        own[span] = added(pair[span], land_high[span])
        yield
    for copy in list(core_copies.values()) + low_copies + high_copies:
        copy.wait_send()
    for column in range(4):

        @pl.when(jnp.logical_not(at_home & (x == column)))
        def gone():
            out_copy(column).wait_send()


FOLD_STEPS = 7


def fold_scratch(rows):
    block = (rows, LANES)
    return [
        pltpu.VMEM((2,) + block, BF16),
        pltpu.VMEM((2,) + block, BF16),
        pltpu.VMEM(block, BF16),
        pltpu.VMEM(block, BF16),
        pltpu.VMEM(block, BF16),
        pltpu.VMEM((4, PART, LANES), BF16),
        pltpu.SemaphoreType.DMA((2, 2, 2)),
        pltpu.SemaphoreType.DMA((2, 2)),
        pltpu.SemaphoreType.DMA((2, 2)),
        pltpu.SemaphoreType.DMA((4,)),
        pltpu.SemaphoreType.DMA((4,)),
    ]


def sum_kernel(in_ref, quarter_ref, all_ref, own, local_sem, send_sem, recv_sem, *scratch):
    grid = Grid()
    fold_barrier(grid)
    fold = fold_steps(grid, in_ref, quarter_ref, own, scratch)
    me = grid.rank(0, 0, 0)
    half_rows = own.shape[0] // 2
    run(fold, 4)
    halves, keeps = [], []
    for half in (0, 1):
        run(fold, 1)
        span = pl.ds(half * half_rows, half_rows)
        keep = pltpu.make_async_copy(own.at[span], all_ref.at[me, span], local_sem.at[half])
        keep.start()
        keeps.append(keep)
        halves.append(gather_half(grid, half, own, all_ref, send_sem, recv_sem))
        run(halves[-1], 1)
        if half == 0:
            run(halves[0], 1)
    for step in range(GATHER_STEPS):
        for half in halves:
            run(half, 1)
    for keep in keeps:
        keep.wait()
    run(fold)


def sum_grads(addends, quarters, number):
    shards, rows, lanes = addends.shape
    return pl.pallas_call(
        sum_kernel,
        out_shape=jax.ShapeDtypeStruct((16, rows, lanes), BF16),
        in_specs=[pl.BlockSpec(memory_space=pltpu.VMEM)] * 2,
        out_specs=pl.BlockSpec(memory_space=pl.ANY),
        scratch_shapes=[
            pltpu.VMEM((rows, lanes), BF16),
            pltpu.SemaphoreType.DMA((2,)),
            pltpu.SemaphoreType.DMA((2, 20)),
            pltpu.SemaphoreType.DMA((2, 20)),
        ]
        + fold_scratch(rows),
        name="sum_grads",
        compiler_params=pltpu.CompilerParams(
            collective_id=number, has_side_effects=True, vmem_limit_bytes=40 << 20
        ),
    )(addends, quarters)


def turn_kernel(first_ref, second_ref, out_ref):
    layer = pl.program_id(0)

    @pl.when(layer == 0)
    def first():
        out_ref[0] = jnp.transpose(first_ref[...].astype(F32).reshape(-1, LANES))

    @pl.when(layer == 1)
    def second():
        out_ref[0] = jnp.transpose(second_ref[...].astype(F32).reshape(-1, LANES))


def turned_parts(gathered, first, count, turn=0):
    layers = len(gathered)

    def spec(own):
        return pl.BlockSpec(
            (16, PART, LANES),
            lambda i, j: (0, first + (jnp.where(i == own, j, own * 0) + turn) % count, 0),
        )

    return pl.pallas_call(
        turn_kernel,
        grid=(layers, count),
        out_shape=jax.ShapeDtypeStruct((layers, LANES, count * 16 * PART), F32),
        in_specs=[spec(own) for own in range(layers)],
        out_specs=pl.BlockSpec((1, LANES, 16 * PART), lambda i, j: (i, 0, j)),
        name="turned_parts",
        compiler_params=pltpu.CompilerParams(vmem_limit_bytes=24 << 20),
    )(*gathered)


def tall_kernel(down_one, down_two, out_one, out_two, down_ref, out_ref):
    layer = pl.program_id(0)

    def put(down_in, out_in):
        down_ref[0] = down_in[...].astype(F32).reshape(16 * PART, LANES)
        for x in range(4):
            for y in range(4):
                out_ref[0, pl.ds(y * HEAD + x * 16, 16)] = out_in[x * 4 + y].astype(F32)

    @pl.when(layer == 0)
    def first():
        put(down_one, out_one)

    @pl.when(layer == 1)
    def second():
        put(down_two, out_two)


def tall_parts(gathered):
    layers = len(gathered)
    width = 4 * LANES

    def step(i, j, own):
        return jnp.where(i == own, j, 0)

    return pl.pallas_call(
        tall_kernel,
        grid=(layers, 4),
        out_shape=[
            jax.ShapeDtypeStruct((layers, 16 * PART, width), F32),
            jax.ShapeDtypeStruct((layers, LANES, width), F32),
        ],
        in_specs=[
            pl.BlockSpec((16, PART, LANES), lambda i, j, own=own: (0, 7 + step(i, j, own), 0))
            for own in range(layers)
        ]
        + [
            pl.BlockSpec(
                (16, 16, LANES), lambda i, j, own=own: (0, OUT_PART * 4 + step(i, j, own), 0)
            )
            for own in range(layers)
        ],
        out_specs=[
            pl.BlockSpec((1, 16 * PART, LANES), lambda i, j: (i, 0, j)),
            pl.BlockSpec((1, LANES, LANES), lambda i, j: (i, 0, j)),
        ],
        name="tall_parts",
        compiler_params=pltpu.CompilerParams(vmem_limit_bytes=24 << 20),
    )(*gathered, *gathered)


SPAN = 1024
ATTEND_WORK = 88


def sort_in(source_ref, order_ref, target_ref, count):
    def body(i, unused):
        start = order_ref[i] * BLK
        target_ref[pl.ds(pl.multiple_of(i * BLK, BLK), BLK), :] = source_ref[
            pl.ds(start, BLK), :
        ]
        return unused

    lax.fori_loop(0, count, body, 0)


def block_numbers(number_ref, first, count, axis):
    if axis == 0:
        return jnp.concatenate(
            [jnp.full((BLK, 1), number_ref[first + i], jnp.int32) for i in range(count)], 0
        )
    lane = lax.broadcasted_iota(jnp.int32, (1, count * BLK), 1) // BLK
    numbers = jnp.zeros((1, count * BLK), jnp.int32)
    for i in range(count):
        numbers = jnp.where(lane == i, number_ref[first + i], numbers)
    return numbers


def far_partner():
    slot = lax.axis_index("ctx")
    return {"ctx": slot + 1 - 2 * (slot % 2)}


def far_copy(source, target, sems):
    return pltpu.make_async_remote_copy(
        src_ref=source,
        dst_ref=target,
        send_sem=sems.at[0],
        recv_sem=sems.at[1],
        device_id=far_partner(),
        device_id_type=MESH,
    )


def attend_steps(tables, q_ref, kv_ref, context_ref, qs, kvs, logs, scratch):
    order_ref, standing_ref, number_ref, other_ref = tables
    tops, totals, sums, sems = scratch
    sort_in(kv_ref, order_ref, kvs.at[0], 32)
    copy = far_copy(kvs.at[0], kvs.at[1], sems)
    copy.start()
    sort_in(q_ref, order_ref, qs, 32)
    tiles = qs.shape[0] // TILE
    row = lax.broadcasted_iota(jnp.int32, (TILE, TILE), 0)
    column = lax.broadcasted_iota(jnp.int32, (TILE, TILE), 1)
    yield 4

    def highest(scores):
        return jnp.max(scores, 1, keepdims=True)

    def weigh(scores, top, keys):
        weights = jnp.exp(scores - top)
        return jnp.sum(weights, 1, keepdims=True), dots(weights.astype(BF16), keys, 1, 0)

    def wide(vector):
        return jnp.broadcast_to(vector, (TILE, 2 * HEAD))

    def own_tile(tile):
        rows = slice(tile * TILE, (tile + 1) * TILE)
        queries, near = qs[rows, :], kvs[0, rows, :]
        parts = [(jnp.where(column <= row, dots(queries, near, 1, 1), NEGATIVE), near)]
        for low in range(0, tile * TILE, SPAN):
            keys = kvs[0, low : min(low + SPAN, tile * TILE), :]
            parts.append((dots(queries, keys, 1, 1), keys))
        top = highest(parts[0][0])
        for scores, keys in parts[1:]:
            top = jnp.maximum(top, highest(scores))
        total, weighted = 0.0, 0.0
        for scores, keys in parts:
            more, product = weigh(scores, top, keys)
            total, weighted = total + more, weighted + product
        tops[rows, :], totals[rows, :], sums[rows, :] = wide(top), wide(total), weighted

    def other_tile(tile, numbers):
        rows = slice(tile * TILE, (tile + 1) * TILE)
        queries = qs[rows, :]
        own = block_numbers(number_ref, tile * TILE // BLK, TILE // BLK, 0)
        half = tile // 4
        keys = kvs[1, half * SPAN : (half + 1) * SPAN, :]
        parts = [(jnp.where(numbers < own, dots(queries, keys, 1, 1), NEGATIVE), keys)]
        if half:
            keys = kvs[1, :SPAN, :]
            parts.append((dots(queries, keys, 1, 1), keys))
        old = tops[rows, :][:, 0:1]
        top = old
        for scores, keys in parts:
            top = jnp.maximum(top, highest(scores))
        scale = jnp.exp(old - top)
        total, weighted = totals[rows, :][:, 0:1] * scale, sums[rows, :] * scale
        for scores, keys in parts:
            more, product = weigh(scores, top, keys)
            total, weighted = total + more, weighted + product
        sums[rows, :] = weighted / total
        logs[rows, :] = wide(top + jnp.log(total))

    for tile in range(tiles):
        own_tile(tile)
        yield tile + 1
    copy.wait_recv()
    for half in (0, 1):
        numbers = block_numbers(other_ref, half * 16, 16, 1)
        for tile in range(half * 4, half * 4 + 4):
            other_tile(tile, numbers)
            yield 4 + 4 * half
    sort_in(sums, standing_ref, context_ref, 32)
    copy.wait_send()


def attend_scratch(rows):
    return [pltpu.VMEM((rows, 2 * HEAD), F32)] * 3 + [pltpu.SemaphoreType.DMA((2,))]


def attend_back_steps(
    tables, qs, kvs, logs, pull_ref, offset_ref, query_grad_ref, pair_grad_ref, scratch
):
    order_ref, standing_ref, number_ref, other_ref = tables
    pulls, offsets, turned, query_sums, pair_sums, away, land, sems = scratch
    sort_in(pull_ref, order_ref, pulls, 32)
    sort_in(offset_ref, order_ref, offsets, 32)
    pair_sums[...] = jnp.zeros_like(pair_sums)
    tiles = qs.shape[0] // TILE
    row = lax.broadcasted_iota(jnp.int32, (TILE, TILE), 0)
    column = lax.broadcasted_iota(jnp.int32, (TILE, TILE), 1)
    lane = lax.broadcasted_iota(jnp.int32, (TILE, 2 * HEAD), 1)
    yield 4

    def tile_part(tile, half, low, count, mask):
        rows = slice(tile * TILE, (tile + 1) * TILE)
        queries, pull = qs[rows, :], pulls[rows, :]
        keys = kvs[half, low : low + count, :]
        scores = dots(keys, queries, 1, 1)
        if mask is not None:
            scores = jnp.where(mask, scores, NEGATIVE)
        probs = jnp.exp(scores - turned[tile, 0:1])
        score_grad = (probs * (dots(keys, pull, 1, 1) - turned[tile, 1:2])).astype(BF16)
        pair_sums[half, low : low + count, :] += dots(score_grad, queries, 1, 0) + dots(
            probs.astype(BF16), pull, 1, 0
        )
        return dots(score_grad, keys, 0, 0)

    def other_tile(tile, numbers):
        rows = slice(tile * TILE, (tile + 1) * TILE)
        turned[tile] = jnp.transpose(
            jnp.where(lane == 0, logs[rows, :], offsets[rows, :])
        )[:8]
        own = block_numbers(number_ref, tile * TILE // BLK, TILE // BLK, 1)
        half = tile // 4
        grads = tile_part(tile, 1, half * SPAN, SPAN, numbers < own)
        if half:
            grads = grads + tile_part(tile, 1, 0, SPAN, None)
        query_sums[rows, :] = grads

    def own_tile(tile):
        rows = slice(tile * TILE, (tile + 1) * TILE)
        grads = query_sums[rows, :] + tile_part(tile, 0, tile * TILE, TILE, row <= column)
        for low in range(0, tile * TILE, SPAN):
            grads = grads + tile_part(tile, 0, low, min(SPAN, tile * TILE - low), None)
        query_sums[rows, :] = grads

    for half in (0, 1):
        numbers = block_numbers(other_ref, half * 16, 16, 0)
        for tile in range(half * 4, half * 4 + 4):
            other_tile(tile, numbers)
            yield 4 + 4 * half
    away[...] = pair_sums[1].astype(BF16)
    copy = far_copy(away, land, sems)
    copy.start()
    for tile in range(tiles):
        own_tile(tile)
        yield tile + 1
    sort_in(query_sums, standing_ref, query_grad_ref, 32)
    copy.wait_recv()
    pair_sums[0] += land[...].astype(F32)
    sort_in(pair_sums.at[0], standing_ref, pair_grad_ref, 32)
    copy.wait_send()


def attend_back_scratch(rows):
    block = (rows, 2 * HEAD)
    return [
        pltpu.VMEM(block, BF16),
        pltpu.VMEM(block, F32),
        pltpu.VMEM((rows // TILE, 8, TILE), F32),
        pltpu.VMEM(block, F32),
        pltpu.VMEM((2,) + block, F32),
        pltpu.VMEM(block, BF16),
        pltpu.VMEM(block, BF16),
        pltpu.SemaphoreType.DMA((2,)),
    ]


def take_turns(work, total, others):
    done = 0
    ran = [0] * len(others)
    for more in work:
        done += more
        for index, (steps, count) in enumerate(others):
            wanted = min(count, 1 + done * (count - 1) // total)
            run(steps, wanted - ran[index])
            ran[index] = wanted
    for steps, count in others:
        run(steps)


def attend_kernel(*refs):
    tables, (q_ref, kv_ref) = refs[:4], refs[4:6]
    context_ref, qs, kvs, logs = refs[6:10]
    Grid().barrier([far_partner()])
    run(attend_steps(tables, q_ref, kv_ref, context_ref, qs, kvs, logs, refs[10:]))


def attend_gather_kernel(*refs):
    tables, (q_ref, kv_ref, own_ref, tall_own) = refs[:4], refs[4:8]
    context_ref, qs, kvs, logs, all_ref, tall_ref = refs[8:14]
    (send_sem, recv_sem, tall_all), refs = refs[14:17], refs[17:]
    grid = Grid()
    grid.barrier([far_partner()] + share_partners())
    all_ref[grid.rank(0, 0, 0)] = own_ref[...]
    gather = gather_steps(grid, own_ref, all_ref, send_sem, recv_sem)
    work = attend_steps(tables, q_ref, kv_ref, context_ref, qs, kvs, logs, refs[2:])
    sharing = share_steps([(tall_own, tall_all)], *refs[:2])
    take_turns(work, ATTEND_WORK, [(gather, GATHER_STEPS), (sharing, 4)])
    stack_tall(tall_all, tall_ref)


def attend(tables, queries, pairs, number, own=None, tall=None):
    rows = queries.shape[0]
    smem, vmem = pl.BlockSpec(memory_space=pltpu.SMEM), pl.BlockSpec(memory_space=pltpu.VMEM)
    given = [queries, pairs]
    shapes = [
        jax.ShapeDtypeStruct((rows, 2 * HEAD), F32),
        jax.ShapeDtypeStruct((rows, 2 * HEAD), BF16),
        jax.ShapeDtypeStruct((2, rows, 2 * HEAD), BF16),
        jax.ShapeDtypeStruct((rows, 2 * HEAD), F32),
    ]
    scratch = []
    if own is not None:
        given += [own, tall]
        shapes.append(jax.ShapeDtypeStruct((16,) + own.shape, own.dtype))
        shapes.append(jax.ShapeDtypeStruct((6 * HEAD, tall.shape[1]), BF16))
        scratch = [pltpu.SemaphoreType.DMA((2, 20)), pltpu.SemaphoreType.DMA((2, 20))]
        scratch += [pltpu.VMEM((4,) + tall.shape, BF16)] + share_sems(1)
    return pl.pallas_call(
        attend_kernel if own is None else attend_gather_kernel,
        out_shape=shapes,
        in_specs=[smem] * 4 + [vmem] * len(given),
        out_specs=[vmem] * len(shapes),
        scratch_shapes=scratch + attend_scratch(rows),
        name="attend",
        compiler_params=pltpu.CompilerParams(
            collective_id=number, has_side_effects=True, vmem_limit_bytes=48 << 20
        ),
    )(*tables, *given)


def attend_back_leave_kernel(*refs):
    tables, given, made = refs[:4], refs[4:14], refs[14:17]
    qs, kvs, logs, pull_ref, offset_ref = given[:5]
    active_ref, context_ref, tall_ref, stream_ref, bias_ref = given[5:]
    query_grad_ref, pair_grad_ref, out_ref = made
    parts, total_rows = refs[17:19]
    scatter_refs, scratch = refs[19:25], refs[25:]
    grid = Grid()
    grid.barrier([far_partner()])
    scatter = leave_steps(
        grid, active_ref, context_ref, tall_ref, stream_ref, bias_ref, out_ref, parts, total_rows,
        scatter_refs,
    )
    work = attend_back_steps(
        tables, qs, kvs, logs, pull_ref, offset_ref, query_grad_ref, pair_grad_ref, scratch
    )
    take_turns(work, ATTEND_WORK, [(scatter, SCATTER_STEPS)])


def attend_back_gather_kernel(*refs):
    tables, given, made = refs[:4], refs[4:10], refs[10:13]
    qs, kvs, logs, pull_ref, offset_ref, own_ref = given
    query_grad_ref, pair_grad_ref, all_ref = made
    local_sem, send_sem, recv_sem = refs[13:16]
    grid = Grid()
    grid.barrier([far_partner()])
    keep = pltpu.make_async_copy(own_ref, all_ref.at[grid.rank(0, 0, 0)], local_sem)
    keep.start()
    gather = gather_steps(grid, own_ref, all_ref, send_sem, recv_sem)
    work = attend_back_steps(
        tables, qs, kvs, logs, pull_ref, offset_ref, query_grad_ref, pair_grad_ref, refs[16:]
    )
    take_turns(work, ATTEND_WORK, [(gather, GATHER_STEPS)])
    keep.wait()


def attend_back(tables, given, number, leaving=None, own=None):
    rows = given[0].shape[0]
    smem, vmem = pl.BlockSpec(memory_space=pltpu.SMEM), pl.BlockSpec(memory_space=pltpu.VMEM)
    shapes = [jax.ShapeDtypeStruct((rows, 2 * HEAD), F32)] * 2
    out_specs = [vmem] * 2
    if leaving is not None:
        kernel = attend_back_leave_kernel
        given = tuple(given) + tuple(leaving)
        own_rows, width = leaving[3].shape
        shapes.append(jax.ShapeDtypeStruct((own_rows, width), BF16))
        out_specs.append(vmem)
        scratch = [
            pltpu.VMEM((16, own_rows, width), BF16),
            pltpu.VMEM((own_rows, width), F32),
        ] + scatter_scratch(own_rows, width)
    else:
        kernel = attend_back_gather_kernel
        given = tuple(given) + (own,)
        shapes.append(jax.ShapeDtypeStruct((16,) + own.shape, own.dtype))
        out_specs.append(pl.BlockSpec(memory_space=pl.ANY))
        scratch = [
            pltpu.SemaphoreType.DMA,
            pltpu.SemaphoreType.DMA((2, 20)),
            pltpu.SemaphoreType.DMA((2, 20)),
        ]
    return pl.pallas_call(
        kernel,
        out_shape=shapes,
        in_specs=[smem] * 4 + [vmem] * len(given),
        out_specs=out_specs,
        scratch_shapes=scratch + attend_back_scratch(rows),
        name="attend_back",
        compiler_params=pltpu.CompilerParams(
            collective_id=number, has_side_effects=True, vmem_limit_bytes=56 << 20
        ),
    )(*tables, *given)


def block_tables(pair_table, z):
    slots = pair_table.shape[0]
    ranks = slots // 2
    index = jnp.arange(slots, dtype=jnp.int32)

    def plane(which):
        pairs = lax.dynamic_slice_in_dim(pair_table.reshape(ranks, 2), which, 1, 1)
        numbers = jnp.concatenate([pairs, 2 * slots - 1 - pairs], 1).reshape(-1)
        standing = jnp.sum((numbers[None, :] < numbers[:, None]).astype(jnp.int32), 1)
        chosen = (standing[None, :] == index[:, None]).astype(jnp.int32)
        order = jnp.sum(chosen * index[None, :], 1)
        return numbers, (order, standing, jnp.sum(chosen * numbers[None, :], 1))

    numbers, own = plane(z)
    return numbers, own + (plane(1 - z)[1][2],)


def rotation(positions):
    freqs = 10000.0 ** (-jnp.arange(0, ROT, 2, dtype=F32) / ROT)
    angles = positions.astype(F32)[:, None] * freqs[None, :]
    rest = ((0, 0), (0, 2 * HEAD - ROT))
    return (
        jnp.pad(jnp.concatenate([jnp.cos(angles)] * 2, -1), rest, constant_values=1.0),
        jnp.pad(jnp.concatenate([jnp.sin(angles)] * 2, -1), rest),
    )


def on_device(
    hidden_in,
    cotangent,
    pair_table,
    norm_gain,
    norm_bias,
    qkv_weight,
    qkv_bias,
    out_weight,
    out_bias,
    up_weight,
    up_bias,
    down_weight,
    down_bias,
):
    layers = norm_gain.shape[0]
    slot = lax.axis_index("ctx")
    shard = lax.axis_index("fsdp")
    rank, z = slot // 2, slot % 2
    width = hidden_in.shape[2]
    quarter = width // 4

    numbers, tables = block_tables(pair_table, z)
    positions = (
        numbers[:, None] * BLK + jnp.arange(BLK, dtype=jnp.int32)[None, :]
    ).reshape(-1)
    cosines, sines = rotation(positions)

    def columns(weight, part):
        return lax.dynamic_slice_in_dim(weight, part * width + rank * HEAD, HEAD, 2)

    wide = jnp.concatenate(
        [columns(qkv_weight, 1), columns(qkv_weight, 2), columns(qkv_weight, 0)]
        + [jnp.zeros((layers, quarter, HEAD), BF16)]
        + [columns(up_weight, part) for part in range(4)],
        2,
    )
    tall = jnp.concatenate(
        [
            lax.dynamic_slice_in_dim(down_weight, rank * HEAD, HEAD, 1),
            lax.dynamic_slice_in_dim(out_weight, (rank % 4) * HEAD, HEAD, 1),
        ],
        1,
    )
    vectors = lax.all_gather(
        jnp.concatenate(
            [
                norm_gain.reshape(layers, -1),
                norm_bias.reshape(layers, -1),
                qkv_bias,
                out_bias,
                up_bias,
                down_bias,
            ],
            1,
        ),
        "fsdp",
        axis=0,
    ).astype(F32)

    scales, wide_biases, last_biases = [], [], []
    for layer in range(layers):
        vector = vectors[:, layer]
        scales.append(
            jnp.transpose(vector[:, 0:1024].reshape(4, 4, 256), (1, 0, 2)).reshape(4, width)
        )
        b_qkv = lax.dynamic_slice_in_dim(
            vector[:, 1024:1792].reshape(3, 16, HEAD), rank, 1, 1
        ).reshape(3, HEAD)
        b_up = lax.dynamic_slice_in_dim(
            vector[:, 2048:3072].reshape(4, 16, HEAD), rank, 1, 1
        ).reshape(4 * HEAD)
        wide_biases.append(
            jnp.concatenate([b_qkv[1], b_qkv[2], b_qkv[0], jnp.zeros((HEAD,), F32), b_up])[None]
        )
        last_biases.append((vector[:, 1792:2048] + vector[:, 3072:3328]).reshape(1, width))

    number = 1
    stream = hidden_in[0].astype(F32)
    saved = []
    wide_all, tall_all = [None] * layers, [None] * layers
    for layer in range(layers):
        if layer == 0:
            *made, wide_all[0] = enter(
                stream, scales[0], wide_biases[0], cosines, sines, wide[0], True, number
            )
        else:
            made = enter(
                stream, scales[layer], wide_biases[layer], cosines, sines, wide_all[layer], False,
                number,
            )
        number += 1
        normed_all, queries, pairs, active, slope = made
        if layer == 0:
            context, queries, pairs, logs, branch_all, tall_all[0] = attend(
                tables, queries, pairs, number, cotangent[0], tall[0]
            )
        else:
            context, queries, pairs, logs = attend(tables, queries, pairs, number)
        number += 1
        saved.append((stream, normed_all, queries, pairs, active, slope, context, logs))
        leaving = (active, context, tall_all[layer], stream, last_biases[layer])
        if layer < layers - 1:
            stream, wide_all[layer + 1], tall_all[layer + 1] = leave(
                *leaving, wide[layer + 1], tall[layer + 1], number
            )
            number += 1

    grad = cotangent[0].astype(F32)
    gathered = [None] * layers
    addends = quarters = folded = None
    for layer in reversed(range(layers)):
        last = layer == layers - 1
        stream, normed_all, queries, pairs, active, slope, context, logs = saved[layer]
        if last:
            pull, offsets, hidden_grad, down_grad, new_quarters, up_raw, up_bias_raw = back_enter(
                branch_all, active, context, slope, normed_all, tall_all[layer]
            )
            query_grad, pair_grad, output = attend_back(
                tables, (queries, pairs, logs, pull, offsets), number, leaving
            )
        else:
            pull, offsets, hidden_grad, down_grad, new_quarters, up_raw, up_bias_raw, folded = (
                back_enter(
                    grad, active, context, slope, normed_all, tall_all[layer], number,
                    (addends, quarters),
                )
            )
            number += 1
            query_grad, pair_grad, gathered[layer + 1] = attend_back(
                tables, (queries, pairs, logs, pull, offsets), number, None, folded
            )
        number += 1
        grad, addends = back_leave(
            (
                query_grad,
                pair_grad,
                hidden_grad,
                normed_all,
                wide_all[layer].reshape(width, 8 * HEAD),
                scales[layer],
                cosines,
                sines,
                stream,
                grad,
                up_raw,
                up_bias_raw,
                down_grad,
            ),
            stream.shape[0],
            width,
            number,
        )
        quarters = new_quarters
        number += 1

    gathered[0] = sum_grads(addends, quarters, number)
    qkv_out = turned_parts(gathered, 0, 3, 2)
    up_out = turned_parts(gathered, 3, 4)
    down_out, out_out = tall_parts(gathered)
    small = jnp.stack(
        [every[:, (OUT_PART + 1) * PART : (OUT_PART + 1) * PART + 7] for every in gathered]
    ).astype(F32)
    sums = jnp.sum(small[:, :, :5], 1)
    gain_out, shift_out, branch_out = sums[:, 0:2], sums[:, 2:4], sums[:, 4]
    qkv_bias_out = jnp.transpose(
        jnp.roll(small[:, :, 5, : 3 * HEAD].reshape(layers, 16, 3, HEAD), 1, 2), (0, 2, 1, 3)
    ).reshape(layers, -1)
    share = qkv_bias_out.shape[1] // 4
    qkv_bias_out = lax.dynamic_slice_in_dim(qkv_bias_out, shard * share, share, 1)
    up_bias_out = lax.dynamic_slice_in_dim(
        small[:, :, 6].reshape(layers, 16, 4, HEAD), shard, 1, 2
    ).reshape(layers, -1)
    return (
        output[None],
        grad[None],
        gain_out,
        shift_out,
        qkv_out,
        qkv_bias_out,
        out_out,
        branch_out,
        up_out,
        up_bias_out,
        down_out,
        branch_out,
    )


def solution(mesh):
    rows = P("fsdp", "ctx", None)
    vector, matrix = P(None, "fsdp"), P(None, "fsdp", None)
    gains = P(None, None, "fsdp")
    params = (gains, gains) + (matrix, vector) * 4
    return jax.shard_map(
        on_device,
        mesh=mesh,
        in_specs=(rows, rows, P()) + params,
        out_specs=(rows, rows) + params,
        check_vma=False,
    )
```

time: 772 us -> 508 us (0.66)
  waiting for transfers between devices: 127 us -> 0 us
  matrix products: 69.3 us -> 0 us
  Pallas kernels: 380 us -> 443 us
  other arithmetic: 61 us -> 2.49 us
  local copies, waits for them, and re-layouts: 90.3 us -> 48.2 us
  between operations: 16.4 us -> 1.71 us
  starting transfers between devices: 12 us -> 0 us
    psum x2 -> x0, waiting for transfers between devices: 125 us -> none  [the longest x1 125 us: on_device(): lax.psum(jnp.concatenate([vector_grad.reshape(layers, -1), biases], 1), (...]
    dot_general x24 -> x0, matrix products: 69.3 us -> none  [the longest x16 43.4 us: dots(): lax.dot_general(a, b, (((da,), (db,)), ((), ())), preferred_element_type=...]
    pallas_call x14 -> x15, Pallas kernels: 380 us -> 443 us  [the longest x2 83 us: attend_back(): pl.pallas_call(kernel, out_shape=shapes, in_specs=[smem] * 4 + [vmem] * l...]
    convert_element_type x9 -> x3, other arithmetic: 31.6 us -> 1.01 us  [the longest x1 0.93 us: on_device(): grad = cotangent[0].astype(F32)]
    transpose x5 -> x1, local copies, waits for them, and re-layouts: 16.4 us -> 0.01 us  [on_device(): jnp.transpose(jnp.roll(small[:, :, 5, :3 * HEAD].reshape(layers, 16, 3, H...]
    pallas_call x1 -> x0, local copies, waits for them, and re-layouts: 11.9 us -> none  [plane_all_gather(): pl.pallas_call(gather_kernel, out_shape=jax.ShapeDtypeStruct((16,) + own....]
    ppermute x6 -> x0, starting transfers between devices: 11.5 us -> none  [swap(): return lax.ppermute(value, 'ctx', pairs)]
    slice x18 -> x4, local copies, waits for them, and re-layouts: 11.3 us -> 0.64 us  [the longest x2 0.61 us: on_device(): gain_out, shift_out, branch_out = (sums[:, 0:2], sums[:, 2:4], sums[:, 4])]
  transfers between devices with their start and end apart: 12 -> 0, of which waited for: 2 -> 0; matrix products, arithmetic and copies ran while one was open for 16% -> 0% of each run, Pallas kernels for 22% -> 0%
where the time goes in v2:
time: 508 us; the launch traced here: 500 us
  Pallas kernels  443 us (87%)
  local copies, waits for them, and re-layouts  48.2 us (9%)
  blocking collectives  5.23 us (1%)
    pallas_call x2, Pallas kernels, attend_back(): pl.pallas_call(kernel, out_shape=shapes, in_specs=[smem] * 4 + [vmem] * l...  83 us
    pallas_call x2, Pallas kernels, back_leave(): pl.pallas_call(back_leave_kernel, out_shape=[jax.ShapeDtypeStruct((rows,...  71.9 us
    pallas_call x1, Pallas kernels, sum_grads(): pl.pallas_call(sum_kernel, out_shape=jax.ShapeDtypeStruct((16, rows, lane...  67.2 us
    pallas_call x2, Pallas kernels, enter(): pl.pallas_call(functools.partial(enter_kernel, shares), out_shape=shapes,...  64.2 us
    pallas_call x2, Pallas kernels, back_enter(): pl.pallas_call(functools.partial(back_enter_kernel, number is not None, f...  57.2 us
    pallas_call x2, Pallas kernels, attend(): pl.pallas_call(attend_kernel if own is None else attend_gather_kernel, ou...  52.9 us
    unnamed x108, local copies, waits for them, and re-layouts  33.4 us
    pallas_call x1, Pallas kernels, leave(): pl.pallas_call(leave_kernel, out_shape=[jax.ShapeDtypeStruct((rows, width...  31.5 us

profile of v2, /device:TPU:32, one launch (start us, length us, event | category | flops | bytes accessed | tf_op | source)
XLA Modules:
  0.0 500.3 jit_solution(17140666835913794597)
XLA Ops:
  6.8 5.2 %all-gather.1 = bf16[4,2,3328]{2,1,0:T(2,128)(2,1)S(1)} all-gather(bf16[1,2,3328]{2,1,0:T(2,128)(2,1)S(1)} %bitcast.83), channel_id=2, replica_groups=mesh['ctx'=32,'fsdp'=4] {'fsdp'}, dimensions={0}, use_global_device_ids=true | all-gather | bytes 66560 | tf_op jit(solution)/shard_map/all_gather | solution.py:1500
  16.1 1.6 constant_dynamic-slice_fusion.8
  19.0 1.3 copy.51
  21.6 1.3 copy.52
  22.9 1.3 pad.9.refs_4_.sin_ref
  24.3 35.2 %enter.2 = (bf16[16,128,1024]{2,1,0:T(8,128)(2,1)}, bf16[2048,128]{1,0:T(8,128)(2,1)S(1)}, bf16[2048,128]{1,0:T(8,128)(2,1)S(1)}, bf16[2048,256]{1,0:T(8,128)(2,...) custom-call(f32[128,1024]{1,0:T(8,128)S(1)} %bitcast_convert_fusion.refs_0_.refs_3_.stream_ref, ...), custom_call_target="tpu_custom_call" | custom-call | tf_op jit(solution)/shard_map/enter/pallas_call | solution.py:470
  60.5 34.1 %attend.2 = (f32[2048,128]{1,0:T(8,128)S(1)}, bf16[2048,128]{1,0:T(8,128)(2,1)S(1)}, bf16[2,2048,128]{2,1,0:T(8,128)(2,1)S(1)}, f32[2048,128]{1,0:T(8,128)S(1)},...) custom-call(s32[32]{0:T(128)S(1)} %get-tuple-element.151.refs_0_, s32[32]{0:T(128)S(1)} %convert_reduce_fusion.3.refs_1_, ...), custom_call_target="tpu_custom_call" | custom-call | tf_op jit(solution)/shard_map/attend/pallas_call | solution.py:1342
  96.6 31.5 %leave.1 = (f32[128,1024]{1,0:T(8,128)S(1)}, bf16[4,256,512]{2,1,0:T(8,128)(2,1)S(1)}, bf16[384,1024]{1,0:T(8,128)(2,1)S(1)}) custom-call(bf16[2048,256]{1,0:T(8,128)(2,1)S(1)} %get-tuple-element.63.refs_0_.refs_1_, f32[2048,128]{1,0:T(8,128)} %copy-done.11, bf16[384,1024]{1,0:T(8,128)(2,1)S(1)} %get-tuple-element.67.refs_2_.refs_5_, ...), custom_call_target="tpu_custom_call" | custom-call | tf_op jit(solution)/shard_map/leave/pallas_call | solution.py:525
  128.2 29.0 %enter.3 = (bf16[16,128,1024]{2,1,0:T(8,128)(2,1)}, bf16[2048,128]{1,0:T(8,128)(2,1)S(1)}, bf16[2048,128]{1,0:T(8,128)(2,1)S(1)}, bf16[2048,256]{1,0:T(8,128)(2,1)S(1)}, f32[2048,256]{1,0:T(8,128)}) custom-call(f32[128,1024]{1,0:T(8,128)S(1)} %get-tuple-element.68.refs_0_.refs_12_.stream_ref, f32[4,1024]{1,0:T(4,128)S(1)} %bitcast.74, ...), custom_call_target="tpu_custom_call" | custom-call | tf_op jit(solution)/shard_map/enter/pallas_call | solution.py:470
  157.3 18.8 %attend.3 = (f32[2048,128]{1,0:T(8,128)S(1)}, bf16[2048,128]{1,0:T(8,128)(2,1)S(1)}, bf16[2,2048,128]{2,1,0:T(8,128)(2,1)S(1)}, f32[2048,128]{1,0:T(8,128)S(1)}) custom-call(s32[32]{0:T(128)S(1)} %get-tuple-element.151.refs_0_, s32[32]{0:T(128)S(1)} %convert_reduce_fusion.3.refs_1_, s32[32]{0:T(128)S(1)} %get-tuple-element.150.refs_2_, ...), custom_call_target="tpu_custom_call" | custom-call | tf_op jit(solution)/shard_map/attend/pallas_call | solution.py:1342
  178.9 17.9 %back_enter.2 = (bf16[2048,128]{1,0:T(8,128)(2,1)S(1)}, f32[2048,128]{1,0:T(8,128)S(1)}, bf16[2048,256]{1,0:T(8,128)(2,1)S(1)}, bf16[4,256,256]{2,1,0:T(8,128)(2...) custom-call(bf16[16,128,1024]{2,1,0:T(8,128)(2,1)} %get-tuple-element.75.refs_0_, ...), custom_call_target="tpu_custom_call" | custom-call | tf_op jit(solution)/shard_map/back_enter/pallas_call | solution.py:658
  202.1 35.3 %attend_back.2 = (f32[2048,128]{1,0:T(8,128)}, f32[2048,128]{1,0:T(8,128)}, bf16[128,1024]{1,0:T(8,128)(2,1)}) custom-call(s32[32]{0:T(128)} %copy-done.40, s32[32]{0:T(128)} %copy-done.38, s32[32]{0:T(128)} %copy-done.39, s32[32]{0:T(128)} %copy-done.41, bf16[2048,128]{1,0:T(8,128)(2,1)} %copy-done.31, bf16[2,2048,128]{2,1,0:T(8,128)(2,1)} %copy-done.24, ...), custom_call_target="tpu_custom_call" | custom-call | tf_op jit(solution)/shard_map/attend_back/pallas_call | solution.py:1416
  237.4 36.0 %back_leave.2 = (f32[128,1024]{1,0:T(8,128)}, bf16[4,832,256]{2,1,0:T(8,128)(2,1)}) custom-call(f32[2048,128]{1,0:T(8,128)} %get-tuple-element.87.query_grad_ref, f32[2048,128]{1,0:T(8,128)} %get-tuple-element.88.pair_grad_ref, bf16[2048,256]{1,0:T(8,128)(2,1)} %copy-done.17, bf16[16,128,1024]{2,1,0:T(8,128)(2,1)} %get-tuple-element.79.refs_4_.normed_ref, ...), custom_call_target="tpu_custom_call" | custom-call | tf_op jit(solution)/shard_map/back_leave/pallas_call | solution.py:782
  274.4 39.3 %back_enter.3 = (bf16[2048,128]{1,0:T(8,128)(2,1)S(1)}, f32[2048,128]{1,0:T(8,128)S(1)}, bf16[2048,256]{1,0:T(8,128)(2,1)S(1)}, bf16[4,256,256]{2,1,0:T(8,128)(2...) custom-call(f32[128,1024]{1,0:T(8,128)S(1)} %copy-done.13, ...), custom_call_target="tpu_custom_call" | custom-call | tf_op jit(solution)/shard_map/back_enter/pallas_call | solution.py:658
  318.7 47.7 %attend_back.3 = (f32[2048,128]{1,0:T(8,128)}, f32[2048,128]{1,0:T(8,128)}, bf16[16,832,256]{2,1,0:T(8,128)(2,1)}) custom-call(s32[32]{0:T(128)} %copy-done.40, s32[32]{0:T(128)} %copy-done.38, s32[32]{0:T(128)} %copy-done.39, s32[32]{0:T(128)} %copy-done.41, bf16[2048,128]{1,0:T(8,128)(2,1)} %copy-done.29, bf16[2,2048,128]{2,1,0:T(8,128)(2,1)} %copy-done.21, ...), custom_call_target="tpu_custom_call" | custom-call | tf_op jit(solution)/shard_map/attend_back/pallas_call | solution.py:1416
  366.4 36.0 %back_leave.3 = (f32[128,1024]{1,0:T(8,128)}, bf16[4,832,256]{2,1,0:T(8,128)(2,1)}) custom-call(f32[2048,128]{1,0:T(8,128)} %get-tuple-element.101.query_grad_ref, f32[2048,128]{1,0:T(8,128)} %get-tuple-element.102.pair_grad_ref, bf16[2048,256]{1,0:T(8,128)(2,1)} %copy-done.16, bf16[16,128,1024]{2,1,0:T(8,128)(2,1)} %get-tuple-element.95.refs_4_.normed_ref, ...), custom_call_target="tpu_custom_call" | custom-call | tf_op jit(solution)/shard_map/back_leave/pallas_call | solution.py:782
  403.2 1.5 copy-done.14
  404.7 67.2 %sum_grads.1.first_ref.down_one.out_one = bf16[16,832,256]{2,1,0:T(8,128)(2,1)S(1)} custom-call(bf16[4,832,256]{2,1,0:T(8,128)(2,1)S(1)} %copy-done.14, bf16[4,64,256]{2,1,0:T(8,128)(2,1)S(1)} %get-tuple-element.110.quarter_ref), custom_call_target="tpu_custom_call" | custom-call | tf_op jit(solution)/shard_map/sum_grads/pallas_call | solution.py:990
  471.9 2.9 copy-done
  477.4 2.9 copy-done.1
  480.3 2.9 copy-done.2
  483.3 4.1 turned_parts.2
  487.4 5.3 %turned_parts.3 = f32[2,256,4096]{2,1,0:T(8,128)} custom-call(bf16[16,832,256]{2,1,0:T(8,128)(2,1)S(1)} %copy-done.1, bf16[16,832,256]{2,1,0:T(8,128)(2,1)S(1)} %copy-done.2), custom_call_target="tpu_custom_call" | custom-call | tf_op jit(solution)/shard_map/turned_parts/pallas_call | solution.py:1030
  492.7 5.3 %tall_parts.1 = (f32[2,1024,1024]{2,1,0:T(8,128)}, f32[2,256,1024]{2,1,0:T(8,128)}) custom-call(bf16[16,832,256]{2,1,0:T(8,128)(2,1)S(1)} %copy-done.1, bf16[16,832,256]{2,1,0:T(8,128)(2,1)S(1)} %copy-done.2, bf16[16,832,256]{2,1,0:T(8,128)(2,1)S(1)} %copy-done.1, bf16[16,832,256]{2,1,0:T(8,128)(2,1)S(1)} %copy-done.2), custom_call_target="tpu_custom_call" | custom-call | tf_op jit(solution)/shard_map/tall_parts/pallas_call | solution.py:1066
  (167 shorter events, 35.0 us)
Async XLA Ops:
  0.6 14.5 %copy-start.19 = (bf16[1,128,1024]{2,1,0:T(8,128)(2,1)S(1)}, bf16[1,128,1024]{2,1,0:T(8,128)(2,1)}, u32[]{:S(2)}) copy-start(bf16[1,128,1024]{2,1,0:T(8,128)(2,1)} %param.14) | copy-start | bytes 786436
  0.7 14.5 %copy-start.43 = (bf16[1,128,1024]{2,1,0:T(8,128)(2,1)S(1)}, bf16[1,128,1024]{2,1,0:T(8,128)(2,1)}, u32[]{:S(2)}) copy-start(bf16[1,128,1024]{2,1,0:T(8,128)(2,1)} %param.13) | copy-start | bytes 786436
  6.1 151.1 %copy-start.38 = (s32[32]{0:T(128)}, s32[32]{0:T(128)S(1)}, u32[]{:S(2)}) copy-start(s32[32]{0:T(128)S(1)} %convert_reduce_fusion.3.refs_1_) | copy-start | bytes 388
  6.5 150.7 %copy-start.41 = (s32[32]{0:T(128)}, s32[32]{0:T(128)S(1)}, u32[]{:S(2)}) copy-start(s32[32]{0:T(128)S(1)} %select_reduce_fusion.refs_3_) | copy-start | bytes 388
  6.7 150.6 %copy-start.39 = (s32[32]{0:T(128)}, s32[32]{0:T(128)S(1)}, u32[]{:S(2)}) copy-start(s32[32]{0:T(128)S(1)} %get-tuple-element.150.refs_2_) | copy-start | bytes 388
  6.7 150.6 %copy-start.40 = (s32[32]{0:T(128)}, s32[32]{0:T(128)S(1)}, u32[]{:S(2)}) copy-start(s32[32]{0:T(128)S(1)} %get-tuple-element.151.refs_0_) | copy-start | bytes 388
  12.8 115.3 %copy-start.35 = (f32[1,4,4,256]{3,1,2,0:T(4,128)}, f32[1,4,4,256]{3,1,2,0:T(4,128)S(1)}, u32[]{:S(2)}) copy-start(f32[1,4,4,256]{3,1,2,0:T(4,128)S(1)} %copy.62) | copy-start | bytes 49156
  13.0 11.3 %copy-start.34 = (f32[1,4,4,256]{3,1,2,0:T(4,128)}, f32[1,4,4,256]{3,1,2,0:T(4,128)S(1)}, u32[]{:S(2)}) copy-start(f32[1,4,4,256]{3,1,2,0:T(4,128)S(1)} %copy.60) | copy-start | bytes 49156
  15.2 81.4 %copy-start.5 = (f32[128,1024]{1,0:T(8,128)}, f32[128,1024]{1,0:T(8,128)S(1)}, u32[]{:S(2)}) copy-start(f32[128,1024]{1,0:T(8,128)S(1)} %bitcast_convert_fusion.refs_0_.refs_3_.stream_ref) | copy-start | bytes 1572868
  21.6 106.6 %copy-start.3 = (f32[2048,128]{1,0:T(8,128)}, f32[2048,128]{1,0:T(8,128)S(1)}, u32[]{:S(2)}) copy-start(f32[2048,128]{1,0:T(8,128)S(1)} %pad.8.refs_3_.cos_ref) | copy-start | bytes 3145732
  22.9 73.6 %copy-start.20 = (bf16[256,512]{1,0:T(8,128)(2,1)S(1)}, bf16[256,512]{1,0:T(8,128)(2,1)}, u32[]{:S(2)}) copy-start(bf16[256,512]{1,0:T(8,128)(2,1)} %get-tuple-element.165.refs_5_) | copy-start | bytes 786436
  24.3 103.9 %copy-start.4 = (f32[2048,128]{1,0:T(8,128)}, f32[2048,128]{1,0:T(8,128)S(1)}, u32[]{:S(2)}) copy-start(f32[2048,128]{1,0:T(8,128)S(1)} %pad.9.refs_4_.sin_ref) | copy-start | bytes 3145732
  60.5 96.8 %copy-start.10 = (bf16[2048,256]{1,0:T(8,128)(2,1)}, bf16[2048,256]{1,0:T(8,128)(2,1)S(1)}, u32[]{:S(2)}) copy-start(bf16[2048,256]{1,0:T(8,128)(2,1)S(1)} %get-tuple-element.63.refs_0_.refs_1_) | copy-start | bytes 3145732
  96.6 31.6 %copy-start.21 = (bf16[2,2048,128]{2,1,0:T(8,128)(2,1)}, bf16[2,2048,128]{2,1,0:T(8,128)(2,1)S(1)}, u32[]{:S(2)}) copy-start(bf16[2,2048,128]{2,1,0:T(8,128)(2,1)S(1)} %get-tuple-element.85.refs_5_) | copy-start | bytes 3145732
  96.6 31.6 %copy-start.29 = (bf16[2048,128]{1,0:T(8,128)(2,1)}, bf16[2048,128]{1,0:T(8,128)(2,1)S(1)}, u32[]{:S(2)}) copy-start(bf16[2048,128]{1,0:T(8,128)(2,1)S(1)} %get-tuple-element.84.refs_4_) | copy-start | bytes 1572868
  128.1 68.8 %copy-start.6 = (f32[128,1024]{1,0:T(8,128)}, f32[128,1024]{1,0:T(8,128)S(1)}, u32[]{:S(2)}) copy-start(f32[128,1024]{1,0:T(8,128)S(1)} %get-tuple-element.68.refs_0_.refs_12_.stream_ref) | copy-start | bytes 1572868
  128.1 68.8 %copy-start.7 = (bf16[4,256,512]{2,1,0:T(8,128)(2,1)}, bf16[4,256,512]{2,1,0:T(8,128)(2,1)S(1)}, u32[]{:S(2)}) copy-start(bf16[4,256,512]{2,1,0:T(8,128)(2,1)S(1)} %get-tuple-element.69.refs_5_) | copy-start | bytes 3145732
  128.1 68.8 %copy-start.12 = (bf16[384,1024]{1,0:T(8,128)(2,1)}, bf16[384,1024]{1,0:T(8,128)(2,1)S(1)}, u32[]{:S(2)}) copy-start(bf16[384,1024]{1,0:T(8,128)(2,1)S(1)} %get-tuple-element.80.refs_5_.refs_11_) | copy-start | bytes 2359300
  157.3 21.7 %copy-start.8 = (bf16[2048,256]{1,0:T(8,128)(2,1)}, bf16[2048,256]{1,0:T(8,128)(2,1)S(1)}, u32[]{:S(2)}) copy-start(bf16[2048,256]{1,0:T(8,128)(2,1)S(1)} %get-tuple-element.76.refs_1_.refs_9_) | copy-start | bytes 3145732
  178.9 18.0 %copy-start.25 = (f32[2048,128]{1,0:T(8,128)}, f32[2048,128]{1,0:T(8,128)S(1)}, u32[]{:S(2)}) copy-start(f32[2048,128]{1,0:T(8,128)S(1)} %get-tuple-element.74.refs_6_) | copy-start | bytes 3145732
  477.4 20.6 %copy-start.45 = (f32[2,1,256]{2,0,1:T(2,128)}, f32[2,1,256]{2,0,1:T(2,128)S(1)}, u32[]{:S(2)}) copy-start(f32[2,1,256]{2,0,1:T(2,128)S(1)} %copy.67) | copy-start | bytes 6148
  477.4 2.9 copy-start.1
  492.6 5.9 %copy-start.44 = (bf16[128,1024]{1,0:T(8,128)(2,1)S(1)}, bf16[128,1024]{1,0:T(8,128)(2,1)}, u32[]{:S(2)}) copy-start(bf16[128,1024]{1,0:T(8,128)(2,1)} %get-tuple-element.83) | copy-start | bytes 786436
  492.7 6.6 %copy-start.42 = (f32[128,1024]{1,0:T(8,128)S(1)}, f32[128,1024]{1,0:T(8,128)}, u32[]{:S(2)}) copy-start(f32[128,1024]{1,0:T(8,128)} %get-tuple-element.108) | copy-start | bytes 1572868
  (22 other events, 24.2 us)
